TPU v7x, 32 devices: a whole 2x2x4 slice. The times are simulated.
32 devices in a mesh: wide: 4 (over y, x), narrow: 8 (over z, core).
Axes of the slice: x: 2, y: 2, z: 4, core: 2. Of those that a mesh axis runs over, the one named last changes fastest.
Arguments:
- coeff: bfloat16 [4096, 2048], P('wide', 'narrow'), may hold values from -6 to 6
- groupb_row_energy: float32 [4096], P('wide'), may hold values from 0.2 to 2
- groupa_energy: float32 [2048], P('narrow'), may hold values from 0.2 to 2
- groupb_basis_values: bfloat16 [4, 1024, 64], replicated, may hold values from -0.1875 to 0.1875
- basis_a: bfloat16 [2048, 2048], replicated, may hold values from -0.125 to 0.125
- potential: float32 [1024, 2048], P(('wide', 'narrow')), may hold values from 0.1 to 3
- slot_sparse_level: int32 [64], P('wide'), may hold values from 0 to 3
- block_pad: int32 [64], P('wide'), may hold values from 0 to 64, as said below
- slot_grid_offset: int32 [64], P('wide'), may hold values from 0 to 1023
Outputs:
- product: float32 [4096, 2048], P('wide', 'narrow')
Inputs may be any that keep to these rules, and one draw needn't show every extreme that they name: `block_pad`: A value of 64 marks an empty slot; one index of wide has all 16 slots filled and another only its first.
All inputs are finite; a program needn't handle non-finite values.
Results may differ from a plain program's by a relative error of at most 0.0023.
Values may be sent and summed in bfloat16 or wider, within the bound.
No kernel may reach another device: no remote copies, remote signals or barrier semaphores. Data moves between devices by JAX's collectives and lax.ppermute only.
A program may use at most 128 MiB of HBM per device.

v0:
```python
import jax
import jax.numpy as jnp
from jax import lax
from jax.sharding import PartitionSpec as P


def rolled_bases(groupb_basis_values, levels, shifts, padding):
    block_width = groupb_basis_values.shape[2]
    grid_count = groupb_basis_values.shape[1]
    doubled = jnp.concatenate((groupb_basis_values, groupb_basis_values), axis=1)

    def one_slot(carry, entry):
        level, shift, pad_rows = entry
        table = lax.dynamic_index_in_dim(doubled, level, 0, keepdims=False)
        rolled = lax.dynamic_slice_in_dim(table, grid_count - shift, grid_count, 0)
        rolled = jnp.where(pad_rows < block_width, rolled, jnp.zeros((), jnp.bfloat16))
        return (carry, rolled)

    _, stacked = lax.scan(one_slot, jnp.int32(0), (levels, shifts, padding))
    return stacked


def forward_sum(operand, level_blocks):
    return lax.dot_general(
        operand, level_blocks, (((0, 2), (0, 1)), ((), ())), preferred_element_type=jnp.float32
    )


def backward_blocks(operand, whole_grid):
    return jnp.einsum("sgj,ga->sja", operand, whole_grid, preferred_element_type=jnp.float32)


def grid_section(partial_value, basis_a, potential):
    summed = lax.psum_scatter(partial_value, "wide", scatter_dimension=0, tiled=True).astype(
        jnp.bfloat16
    )
    by_rows = lax.all_to_all(summed, "narrow", split_axis=0, concat_axis=1, tiled=True)
    on_grid = jnp.dot(by_rows, basis_a, preferred_element_type=jnp.float32)
    acted = (potential * on_grid).astype(jnp.bfloat16)
    returned = lax.dot_general(
        acted, basis_a, (((1,), (1,)), ((), ())), preferred_element_type=jnp.float32
    ).astype(jnp.bfloat16)
    by_columns = lax.all_to_all(returned, "narrow", split_axis=1, concat_axis=0, tiled=True)
    return lax.all_gather(by_columns, "wide", axis=0, tiled=True)


def body(
    coeff,
    groupb_row_energy,
    groupa_energy,
    groupb_basis_values,
    basis_a,
    potential,
    slot_sparse_level,
    block_pad,
    slot_grid_offset,
):
    block_width = groupb_basis_values.shape[2]
    slot_count = block_pad.shape[0]
    columns = coeff.shape[1]
    level_blocks = coeff.reshape(slot_count, block_width, columns)
    alive_rows = jnp.arange(block_width)[None, :] < (block_width - block_pad)[:, None]
    masked = jnp.where(alive_rows[:, :, None], level_blocks, jnp.zeros((), jnp.bfloat16))
    operand = rolled_bases(groupb_basis_values, slot_sparse_level, slot_grid_offset, block_pad)
    partial_value = forward_sum(operand, masked)
    whole_grid = grid_section(partial_value, basis_a, potential)
    results = backward_blocks(operand, whole_grid)
    diagonal_energy = (
        groupb_row_energy.reshape(slot_count, block_width)[:, :, None]
        + groupa_energy[None, None, :]
    )
    hamiltonian_output = jnp.where(
        alive_rows[:, :, None],
        diagonal_energy * level_blocks.astype(jnp.float32) + results,
        jnp.float32(0.0),
    )
    return hamiltonian_output.reshape(slot_count * block_width, columns)


def solution(mesh):
    return jax.shard_map(
        body,
        mesh=mesh,
        in_specs=(
            P("wide", "narrow"),
            P("wide"),
            P("narrow"),
            P(),
            P(),
            P(("wide", "narrow"), None),
            P("wide"),
            P("wide"),
            P("wide"),
        ),
        out_specs=P("wide", "narrow"),
        check_vma=False,
    )
```

profile of v0, /device:TPU:0, one launch (start us, length us, event | category | flops | bytes accessed | tf_op | source)
XLA Modules:
  0.0 200.8 jit_solution(10285204198233650143)
XLA Ops:
  6.5 1.5 copy.21
  8.6 102.7 %while.13 = (s32[]{:T(128)}, bf16[16,1024,64]{2,1,0:T(8,128)(2,1)}, s32[16]{0:T(128)S(1)}, s32[16]{0:T(128)S(1)}, s32[16]{0:T(128)S(1)}, /*index=5*/bf16[4,2048,...) while((s32[]{:T(128)}, bf16[16,1024,64]{2,1,0:T(8,128)(2,1)}, ...), condition=%wide.region_1.2_spmd, body=%wide.region_0.1_spmd.sunk | while | flops 65548 | bytes 394538 | solution.py:19
  14.2 0.8 select_dynamic-update-slice_fusion.2
  20.6 0.8 select_dynamic-update-slice_fusion.2
  39.8 0.8 select_dynamic-update-slice_fusion.2
  46.3 0.8 select_dynamic-update-slice_fusion.2
  52.7 0.8 select_dynamic-update-slice_fusion.2
  59.1 0.8 select_dynamic-update-slice_fusion.2
  65.5 0.8 select_dynamic-update-slice_fusion.2
  72.0 0.8 select_dynamic-update-slice_fusion.2
  78.4 0.8 select_dynamic-update-slice_fusion.2
  84.8 0.8 select_dynamic-update-slice_fusion.2
  91.2 0.8 select_dynamic-update-slice_fusion.2
  97.6 0.8 select_dynamic-update-slice_fusion.2
  104.0 0.8 select_dynamic-update-slice_fusion.2
  111.3 4.4 %convolution_bitcast_fusion = f32[1024,256]{1,0:T(8,128)} fusion(bf16[16,1024,64]{2,1,0:T(8,128)(2,1)} %get-tuple-element.103, bf16[16,64,256]{2,1,0:T(8,128)(2,1)} %bitcast.37, pred[16,64]{1,0:T(8,128)(4,1)S(1)} %iota_compare_fusion), kind=kOutput, calls=%fused_computation.7 | convolution fusion | flops 537133056 | bytes 3671040 | tf_op jit(solution)/shard_map/dot_general | solution.py:24
  115.7 30.6 %reduce-scatter.2.cloned.1.call-done = f32[256,256]{1,0:T(8,128)} async-done(((f32[1024,256]{1,0:T(8,128)}), f32[256,256]{1,0:T(8,128)}) %reduce-scatter.2.cloned.1.call-update) | async-done | bytes 262160 | tf_op jit(solution)/shard_map/reduce_scatter | solution.py:34
  146.3 1.0 convert_element_type.13
  147.3 11.2 %all_to_all.38 = bf16[8,32,256]{2,1,0:T(8,128)(2,1)S(1)} all-to-all(bf16[8,32,256]{2,1,0:T(8,128)(2,1)S(1)} %bitcast.40), channel_id=1, replica_groups=mesh['wide'=4,'narrow'=8] {'narrow'}, dimensions={0} | all-to-all | bytes 262144 | tf_op jit(solution)/shard_map/all_to_all | solution.py:37
  158.5 9.9 %convolution_convert_fusion = bf16[32,2048]{1,0:T(8,128)(2,1)S(1)} fusion(bf16[2048,2048]{1,0:T(8,128)(2,1)} %param.15, f32[32,2048]{1,0:T(8,128)S(1)} %copy-done.1, bf16[32,2048]{1,0:T(8,128)(2,1)S(1)} %bitcast.35), kind=kOutput, calls=%fused_computation.3 | convolution fusion | flops 537067520 | bytes 8912896 | tf_op jit(solution)/shard_map/dot_general | solution.py:40
  169.1 3.4 %all-to-all-start.1 = ((bf16[32,8,256]{2,0,1:T(8,128)(2,1)}), bf16[32,8,256]{2,0,1:T(8,128)(2,1)S(1)}, u32[]{:S(2)}, u32[]{:S(2)}) async-start(bf16[32,8,256]{2,0,1:T(8,128)(2,1)} %bitcast.26), calls=%async_computation.2 | async-start | bytes 262144 | tf_op jit(solution)/shard_map/all_to_all | solution.py:43
  172.5 6.6 %all-to-all-done.1 = bf16[32,8,256]{2,0,1:T(8,128)(2,1)S(1)} async-done(((bf16[32,8,256]{2,0,1:T(8,128)(2,1)}), bf16[32,8,256]{2,0,1:T(8,128)(2,1)S(1)}, u32[]{:S(2)}, u32[]{:S(2)}) %all-to-all-start.1) | async-done | bytes 131104 | tf_op jit(solution)/shard_map/all_to_all | solution.py:43
  179.2 10.2 %all_gather.3 = bf16[1024,256]{1,0:T(8,128)(2,1)S(1)} all-gather(bf16[256,256]{1,0:T(8,128)(2,1)S(1)} %bitcast.39), channel_id=1, replica_groups=mesh['wide'=4,'narrow'=8] {'wide'}, dimensions={0}, use_global_device_ids=true | all-gather | bytes 655360 | tf_op jit(solution)/shard_map/all_gather | solution.py:44
  189.4 4.6 %fusion.1 = f32[16,64,256]{2,1,0:T(8,128)} fusion(bf16[16,1024,64]{2,1,0:T(8,128)(2,1)} %get-tuple-element.103, bf16[16,64,256]{2,1,0:T(8,128)(2,1)S(1)} %bitcast.38, bf16[1024,256]{1,0:T(8,128)(2,1)S(1)} %all_gather.3, f32[256]{0:T(256)S(1)} %copy-done.3, f32[16,64]{1,0:T(8,128)S(1)} %add.52, pred[16,64]{1,0:T(8,128)(4,1)S(1)} %iota_compare_fusion), kind=kOutput, calls=%fused_computation.6 | convolution fusion | flops 538181632 | bytes 4200448 | tf_op jit(solution)/shard_map/sgj,ga->sja/dot_general | solution.py:30
  (74 shorter events, 33.1 us)
Async XLA Ops:
  6.5 2.0 copy-start.4
  6.5 2.0 copy-start.5
  6.5 2.0 %copy-start.6 = (s32[16]{0:T(128)S(1)}, s32[16]{0:T(128)}, u32[]{:S(2)}) copy-start(s32[16]{0:T(128)} %param.19) | copy-start | bytes 196
  6.5 139.8 %reduce-scatter.2.cloned.1.call-start = ((), (), s32[]{:S(2)}) async-start(), calls=%async_computation.3 | async-start | bytes 1310720 | tf_op jit(solution)/shard_map/reduce_scatter | solution.py:34
  111.3 47.1 %copy-start.1 = (f32[32,2048]{1,0:T(8,128)S(1)}, f32[32,2048]{1,0:T(8,128)}, u32[]{:S(2)}) copy-start(f32[32,2048]{1,0:T(8,128)} %param.16) | copy-start | bytes 786436
  158.5 14.0 %copy-start.2 = (f32[1024]{0:T(1024)S(1)}, f32[1024]{0:T(1024)}, u32[]{:S(2)}) copy-start(f32[1024]{0:T(1024)} %param.12) | copy-start | bytes 12292
  158.5 30.9 %copy-start = (bf16[1024,256]{1,0:T(8,128)(2,1)S(1)}, bf16[1024,256]{1,0:T(8,128)(2,1)}, u32[]{:S(2)}) copy-start(bf16[1024,256]{1,0:T(8,128)(2,1)} %param.11) | copy-start | bytes 1572868
  158.5 30.9 %copy-start.3 = (f32[256]{0:T(256)S(1)}, f32[256]{0:T(256)}, u32[]{:S(2)}) copy-start(f32[256]{0:T(256)} %param.13) | copy-start | bytes 3076
  169.1 10.1 %all-to-all-start.1 = ((bf16[32,8,256]{2,0,1:T(8,128)(2,1)}), bf16[32,8,256]{2,0,1:T(8,128)(2,1)S(1)}, u32[]{:S(2)}, u32[]{:S(2)}) async-start(bf16[32,8,256]{2,0,1:T(8,128)(2,1)} %bitcast.26), calls=%async_computation.2 | async-start | bytes 262144 | tf_op jit(solution)/shard_map/all_to_all | solution.py:43
Sparse Core Ops, SparseCore 0:
  115.8 30.4 reduce-scatter.1
where the time goes:
time: 202 us; the launch traced here: 201 us
  loops' own time  60.4 us (30%)
  waiting for transfers between devices  37.2 us (18%)
  local copies, waits for them, and re-layouts  31.8 us (16%)
  blocking collectives  21.4 us (11%)
  matrix products  18.8 us (9%)
  other arithmetic  14.3 us (7%)
  between operations  13.5 us (7%)
  starting transfers between devices  3.37 us (2%)
    another operation x1, loops' own time, rolled_bases(): _, stacked = lax.scan(one_slot, jnp.int32(0), (levels, shifts, padding))  60.4 us
    reduce_scatter x1, waiting for transfers between devices, grid_section(): lax.psum_scatter(partial_value, 'wide', scatter_dimension=0, tiled=True)  30.6 us
    dynamic_slice x48, local copies, waits for them, and re-layouts, rolled_bases(): _, stacked = lax.scan(one_slot, jnp.int32(0), (levels, shifts, padding))  29.4 us
    dynamic_update_slice x16, other arithmetic, rolled_bases(): _, stacked = lax.scan(one_slot, jnp.int32(0), (levels, shifts, padding))  12.8 us
    all_to_all x1, blocking collectives, grid_section(): lax.all_to_all(summed, 'narrow', split_axis=0, concat_axis=1, tiled=True)  11.2 us
    all_gather x1, blocking collectives, grid_section(): return lax.all_gather(by_columns, 'wide', axis=0, tiled=True)  10.2 us
    dot_general x1, matrix products, grid_section(): lax.dot_general(acted, basis_a, (((1,), (1,)), ((), ())), preferred_eleme...  9.86 us
    all_to_all x1, waiting for transfers between devices, grid_section(): lax.all_to_all(returned, 'narrow', split_axis=1, concat_axis=0, tiled=True)  6.63 us
  transfers between devices with their start and end apart: 2, of which 2 were waited for; matrix products, arithmetic and copies ran while one was open for 0% of the time, Pallas kernels for 0%

commit v1 on v0

v1 whole, which is shorter than its diff:
```python
import functools

import jax
import jax.numpy as jnp
from jax import lax
from jax.experimental import pallas as pl
from jax.experimental.pallas import tpu as pltpu
from jax.sharding import PartitionSpec as P

MIB = 1024 * 1024
HBM = pl.BlockSpec(memory_space=pltpu.HBM)
VMEM = pl.BlockSpec(memory_space=pltpu.VMEM)
BF16 = jnp.bfloat16
F32 = jnp.float32


def call(kernel, name, out_shape, in_specs, out_specs, scratch=(), flops=0, moved=0, mib=16):
    return pl.pallas_call(
        kernel,
        out_shape=out_shape,
        in_specs=in_specs,
        out_specs=out_specs,
        scratch_shapes=scratch,
        compiler_params=pltpu.CompilerParams(vmem_limit_bytes=mib * MIB),
        cost_estimate=pl.CostEstimate(flops=flops, bytes_accessed=moved, transcendentals=0),
        name=name,
    )


def in_hbm(value):
    return pltpu.with_memory_space_constraint(value, pltpu.HBM)


def array(shape, dtype):
    return jax.ShapeDtypeStruct(shape, dtype)


def dot(left, right):
    return jnp.dot(left, right, preferred_element_type=F32)


def dot_turned(left, right):
    return lax.dot_general(left, right, (((1,), (1,)), ((), ())), preferred_element_type=F32)


def first_kernel(
    wide,
    chips,
    level_hbm,
    pad_hbm,
    shift_hbm,
    coeff_hbm,
    table_hbm,
    basis_hbm,
    potential_hbm,
    out_ref,
    turned_ref,
    rolled_ref,
    basis_ref,
    potential_ref,
    level_ref,
    pad_ref,
    shift_ref,
    coeff_ref,
    table_ref,
    sems,
):
    place = lax.axis_index("narrow")
    core, chip = place % 2, place // 2
    columns = coeff_ref.shape[1]
    pairs = [
        (level_hbm, level_ref),
        (shift_hbm, shift_ref),
        (pad_hbm, pad_ref),
        (table_hbm, table_ref),
        (coeff_hbm, coeff_ref),
        (potential_hbm, potential_ref),
    ]
    for j in range(chips):
        start = pl.multiple_of(((chip ^ j) * 2 + core) * columns, columns)
        pairs.append((basis_hbm.at[pl.ds(start, columns), :], basis_ref.at[j]))
    copies = [
        pltpu.make_async_copy(source, target, sems.at[i])
        for i, (source, target) in enumerate(pairs)
    ]
    for copy in copies:
        copy.start()
    for copy in copies[:4]:
        copy.wait()
    slots = pad_ref.shape[0]
    width = table_ref.shape[1]
    for s in range(slots):
        rows = slice(s * width, (s + 1) * width)
        table = table_ref[level_ref[s]].astype(F32)
        rolled_ref[rows, :] = pltpu.roll(table, shift_ref[s], 1).astype(BF16)
    copies[4].wait()
    row = lax.broadcasted_iota(jnp.int32, (width, columns), 0)
    pieces = []
    for s in range(slots):
        rows = slice(s * width, (s + 1) * width)
        piece = coeff_ref[rows, :].astype(F32)
        pieces.append(jnp.where(row < width - pad_ref[s], piece, 0.0))
    turned_ref[...] = jnp.concatenate(pieces, axis=0).T.astype(BF16)
    me = lax.axis_index("wide")
    own = rolled_ref.shape[1] // wide
    start = pl.multiple_of((me ^ (wide - 1)) * own, own)
    total = dot(turned_ref[...], rolled_ref[:, pl.ds(start, own)])
    out_ref[...] = total.T.astype(BF16)
    for copy in copies[5:]:
        copy.wait()


def first(wide, chips, level, pad, shift, coeff, tables, basis, potential):
    rows, columns = coeff.shape
    points = tables.shape[2]
    own = points // wide
    slots = pad.shape[0]
    inputs = (level, pad, shift, coeff, tables, basis, potential)
    return call(
        functools.partial(first_kernel, wide, chips),
        "forward_first",
        (
            array((own, columns), BF16),
            array((columns, rows), BF16),
            array((rows, points), BF16),
            array((chips, columns, basis.shape[1]), BF16),
            array(potential.shape, F32),
        ),
        [HBM] * 7,
        (VMEM,) * 5,
        [
            pltpu.SMEM((slots,), jnp.int32),
            pltpu.SMEM((slots,), jnp.int32),
            pltpu.SMEM((slots,), jnp.int32),
            pltpu.VMEM(coeff.shape, coeff.dtype),
            pltpu.VMEM(tables.shape, tables.dtype),
            pltpu.SemaphoreType.DMA((6 + chips,)),
        ],
        flops=2 * rows * own * columns,
        moved=8 * MIB,
    )(*(in_hbm(value) for value in inputs))


def second_kernel(wide, turned_ref, rolled_ref, *outs):
    me = lax.axis_index("wide")
    own = rolled_ref.shape[1] // wide
    for k in range(wide - 1):
        start = pl.multiple_of((me ^ k) * own, own)
        total = dot(turned_ref[...], rolled_ref[:, pl.ds(start, own)])
        outs[k][...] = total.T.astype(outs[k].dtype)


def second(wide, turned, rolled):
    columns, rows = turned.shape
    own = rolled.shape[1] // wide
    return call(
        functools.partial(second_kernel, wide),
        "forward_rest",
        tuple(array((own, columns), BF16 if k else F32) for k in range(wide - 1)),
        [VMEM] * 2,
        (VMEM,) * (wide - 1),
        flops=2 * rows * own * columns * (wide - 1),
        moved=3 * MIB,
    )(turned, rolled)


def combine_kernel(wide, chips, *refs):
    parts, outs = refs[:wide], refs[wide:]
    chip = lax.axis_index("narrow") // 2
    rows = outs[0].shape[0]
    for j in range(chips):
        start = pl.multiple_of((chip ^ j) * rows, rows)
        total = parts[0][pl.ds(start, rows), :]
        for part in parts[1:]:
            total = total + part[pl.ds(start, rows), :].astype(F32)
        outs[j][...] = total.astype(BF16)


def combine(chips, parts):
    rows, columns = parts[0].shape
    wide = len(parts)
    return call(
        functools.partial(combine_kernel, wide, chips),
        "wide_sum",
        tuple(array((rows // chips, columns), BF16) for _ in range(chips)),
        [VMEM] * wide,
        (VMEM,) * chips,
        moved=MIB,
    )(*parts)


def early_kernel(x_ref, basis_ref, out_ref):
    out_ref[...] = dot(x_ref[...], basis_ref[0])


def early(x, basis):
    rows = x.shape[0]
    points = basis.shape[2]
    return call(
        early_kernel,
        "points_own",
        array((rows, points), F32),
        [VMEM] * 2,
        VMEM,
        flops=2 * rows * points * x.shape[1],
        moved=2 * MIB,
    )(x, basis)


def points_kernel(chips, total_ref, *refs):
    xs = refs[: chips - 1]
    basis_ref, mine_ref, theirs_ref, sum_ref = refs[chips - 1 :]
    core = lax.axis_index("narrow") % 2
    rows = mine_ref.shape[0]
    points = mine_ref.shape[1]
    step = min(points, 512)
    for p in range(0, points, step):
        span = slice(p, p + step)
        total = total_ref[:, span]
        for j in range(1, chips):
            total = total + dot(xs[j - 1][...], basis_ref[j, :, span])
        sum_ref[:, span] = total
    mine_ref[...] = sum_ref[pl.ds(pl.multiple_of(core * rows, rows), rows), :]
    theirs_ref[...] = sum_ref[pl.ds(pl.multiple_of((1 - core) * rows, rows), rows), :]


def to_points(total, xs, basis):
    rows, points = total.shape
    half = array((rows // 2, points), F32)
    chips = len(xs) + 1
    return call(
        functools.partial(points_kernel, chips),
        "points_rest",
        (half, half),
        [VMEM] * (chips + 1),
        (VMEM, VMEM),
        [pltpu.VMEM((rows, points), F32)],
        flops=2 * rows * points * xs[0].shape[1] * (chips - 1),
        moved=4 * MIB,
    )(total, *xs, basis)


def act_kernel(mine_ref, other_ref, potential_ref, out_ref):
    on_grid = mine_ref[...] + other_ref[...]
    out_ref[...] = (potential_ref[...] * on_grid).astype(BF16)


def act(mine, other, potential):
    return call(
        act_kernel, "act", array(mine.shape, BF16), [VMEM] * 3, VMEM, moved=MIB
    )(mine, other, potential)


def back_kernel(chips, mine_ref, other_ref, basis_ref, *refs):
    outs, both_ref, rows_ref = refs[:chips - 1], refs[chips - 1], refs[chips]
    core = lax.axis_index("narrow") % 2
    rows = mine_ref.shape[0]
    rows_ref[pl.ds(pl.multiple_of(core * rows, rows), rows), :] = mine_ref[...].astype(F32)
    rows_ref[pl.ds(pl.multiple_of((1 - core) * rows, rows), rows), :] = other_ref[...].astype(F32)
    both_ref[...] = rows_ref[...].astype(BF16)
    for j in range(1, chips):
        outs[j - 1][...] = dot_turned(both_ref[...], basis_ref[j]).astype(BF16)


def to_functions(mine, other, basis):
    rows, points = mine.shape
    chips, columns, _ = basis.shape
    return call(
        functools.partial(back_kernel, chips),
        "functions_rest",
        tuple(array((2 * rows, columns), BF16) for _ in range(chips - 1))
        + (array((2 * rows, points), BF16),),
        [VMEM] * 3,
        (VMEM,) * chips,
        [pltpu.VMEM((2 * rows, points), F32)],
        flops=4 * rows * points * columns * (chips - 1),
        moved=4 * MIB,
    )(mine, other, basis)


def late_kernel(both_ref, basis_ref, out_ref):
    out_ref[...] = dot_turned(both_ref[...], basis_ref[0]).astype(BF16)


def late(both, basis):
    rows, points = both.shape
    columns = basis.shape[1]
    return call(
        late_kernel,
        "functions_own",
        array((rows, columns), BF16),
        [VMEM] * 2,
        VMEM,
        flops=2 * rows * points * columns,
        moved=2 * MIB,
    )(both, basis)


def assemble_kernel(*refs):
    parts, out_ref = refs[:-1], refs[-1]
    chip = lax.axis_index("narrow") // 2
    rows = parts[0].shape[0]
    for j, part in enumerate(parts):
        start = pl.multiple_of((chip ^ j) * rows, rows)
        out_ref[pl.ds(start, rows), :] = part[...]


def assemble(parts):
    rows, columns = parts[0].shape
    chips = len(parts)
    return call(
        assemble_kernel,
        "assemble",
        array((rows * chips, columns), BF16),
        [VMEM] * chips,
        VMEM,
        moved=MIB // 4,
    )(*parts)


def own_kernel(wide, pad_ref, rolled_ref, grid_ref, coeff_ref, row_ref, column_ref, out_ref):
    slots = pad_ref.shape[0]
    width = rolled_ref.shape[0] // slots
    me = lax.axis_index("wide")
    own = rolled_ref.shape[1] // wide
    start = pl.multiple_of(me * own, own)
    out_ref[...] = dot(rolled_ref[:, pl.ds(start, own)], grid_ref[...])
    for s in range(slots):
        rows = slice(s * width, (s + 1) * width)
        energy = row_ref[rows, :] + column_ref[...]
        out_ref[rows, :] += energy * coeff_ref[rows, :].astype(F32)


def backward_own(wide, pad, rolled, grid, coeff, row_energy, column_energy):
    smem = pl.BlockSpec(memory_space=pltpu.SMEM)
    rows, columns = coeff.shape
    return call(
        functools.partial(own_kernel, wide),
        "backward_own",
        array(coeff.shape, F32),
        [smem] + [VMEM] * 5,
        VMEM,
        flops=2 * rows * columns * rolled.shape[1] // wide,
        moved=4 * MIB,
    )(pad, rolled, grid, coeff, row_energy[:, None], column_energy[None, :])


def rest_kernel(wide, pad_ref, total_ref, rolled_ref, *refs):
    grids, (out_hbm, out_ref, sems) = refs[: wide - 1], refs[wide - 1 :]
    slots = pad_ref.shape[0]
    width = rolled_ref.shape[0] // slots
    me = lax.axis_index("wide")
    own = rolled_ref.shape[1] // wide
    starts = [pl.multiple_of((me ^ k) * own, own) for k in range(wide)]
    steps = sems.shape[0]
    rows = rolled_ref.shape[0] // steps
    row = lax.broadcasted_iota(jnp.int32, (width, out_ref.shape[1]), 0)
    copies = []
    for i in range(steps):
        span = pl.ds(i * rows, rows)
        total = total_ref[span, :]
        for k in range(1, wide):
            total = total + dot(rolled_ref[span, pl.ds(starts[k], own)], grids[k - 1][...])
        for s in range(rows // width):
            slot = i * (rows // width) + s
            value = total[s * width : (s + 1) * width, :]
            out_ref[pl.ds(slot * width, width), :] = jnp.where(
                row < width - pad_ref[slot], value, 0.0
            )
        copies.append(pltpu.make_async_copy(out_ref.at[span, :], out_hbm.at[span, :], sems.at[i]))
        copies[-1].start()
    for copy in copies:
        copy.wait()


def backward_rest(wide, pad, total, rolled, grids):
    smem = pl.BlockSpec(memory_space=pltpu.SMEM)
    rows, columns = total.shape
    return call(
        functools.partial(rest_kernel, wide),
        "backward_rest",
        array(total.shape, F32),
        [smem] + [VMEM] * (wide + 1),
        HBM,
        [pltpu.VMEM(total.shape, F32), pltpu.SemaphoreType.DMA((4,))],
        flops=2 * rows * columns * rolled.shape[1],
        moved=4 * MIB,
    )(pad, total, rolled, *grids)


def exchange(value, step, size, axis):
    return lax.ppermute(value, axis, [(i, i ^ step) for i in range(size)])


def body(
    wide,
    narrow,
    coeff,
    groupb_row_energy,
    groupa_energy,
    groupb_basis_values,
    basis_a,
    potential,
    slot_sparse_level,
    block_pad,
    slot_grid_offset,
):
    chips = narrow // 2
    tables = jnp.swapaxes(groupb_basis_values, 1, 2)
    far, turned, rolled, basis, pot = first(
        wide,
        chips,
        slot_sparse_level,
        block_pad,
        slot_grid_offset,
        coeff,
        tables,
        basis_a,
        potential,
    )
    arrived = {wide - 1: exchange(far, wide - 1, wide, "wide")}
    parts = second(wide, turned, rolled)
    for k in range(1, wide - 1):
        arrived[k] = exchange(parts[k], k, wide, "wide")
    pieces = combine(chips, [parts[0]] + [arrived[k] for k in range(1, wide)])
    xs = [exchange(pieces[j], 2 * j, narrow, "narrow") for j in range(1, chips)]
    total = early(pieces[0], basis)
    mine, theirs = to_points(total, xs, basis)
    acted = act(mine, exchange(theirs, 1, narrow, "narrow"), pot)
    other = exchange(acted, 1, narrow, "narrow")
    *blocks, both = to_functions(acted, other, basis)
    sent = [exchange(blocks[j - 1], 2 * j, narrow, "narrow") for j in range(1, chips)]
    grid = assemble([late(both, basis)] + sent)
    grids = [exchange(grid, k, wide, "wide") for k in range(1, wide)]
    start = backward_own(
        wide, block_pad, rolled, grid, coeff, groupb_row_energy, groupa_energy
    )
    return backward_rest(wide, block_pad, start, rolled, grids)


def solution(mesh):
    return jax.shard_map(
        functools.partial(body, mesh.shape["wide"], mesh.shape["narrow"]),
        mesh=mesh,
        in_specs=(
            P("wide", "narrow"),
            P("wide"),
            P("narrow"),
            P(),
            P(),
            P(("wide", "narrow"), None),
            P("wide"),
            P("wide"),
            P("wide"),
        ),
        out_specs=P("wide", "narrow"),
        check_vma=False,
    )
```

time: 202 us -> 46.3 us (0.23)
  loops' own time: 60.4 us -> 0 us
  local copies, waits for them, and re-layouts: 31.8 us -> 0.24 us
  blocking collectives: 21.4 us -> 0 us
  matrix products: 18.8 us -> 0 us
  waiting for transfers between devices: 37.2 us -> 19.2 us
  other arithmetic: 14.3 us -> 0 us
  starting transfers between devices: 3.37 us -> 17.3 us
  between operations: 13.5 us -> 0.14 us
  Pallas kernels: 0 us -> 9.3 us
    another operation x1 -> x0, loops' own time: 60.4 us -> none  [rolled_bases(): _, stacked = lax.scan(one_slot, jnp.int32(0), (levels, shifts, padding))]
    reduce_scatter x1 -> x0, waiting for transfers between devices: 30.6 us -> none  [grid_section(): lax.psum_scatter(partial_value, 'wide', scatter_dimension=0, tiled=True)]
    dynamic_slice x48 -> x0, local copies, waits for them, and re-layouts: 29.4 us -> none  [rolled_bases(): _, stacked = lax.scan(one_slot, jnp.int32(0), (levels, shifts, padding))]
    ppermute x0 -> x14, waiting for transfers between devices: none -> 19.2 us  [exchange(): return lax.ppermute(value, axis, [(i, i ^ step) for i in range(size)])]
    dot_general x3 -> x0, matrix products: 18.8 us -> none  [the longest x1 9.86 us: grid_section(): lax.dot_general(acted, basis_a, (((1,), (1,)), ((), ())), preferred_eleme...]
    ppermute x0 -> x14, starting transfers between devices: none -> 17.3 us  [exchange(): return lax.ppermute(value, axis, [(i, i ^ step) for i in range(size)])]
    dynamic_update_slice x16 -> x0, other arithmetic: 12.8 us -> none  [rolled_bases(): _, stacked = lax.scan(one_slot, jnp.int32(0), (levels, shifts, padding))]
    all_to_all x1 -> x0, blocking collectives: 11.2 us -> none  [grid_section(): lax.all_to_all(summed, 'narrow', split_axis=0, concat_axis=1, tiled=True)]
  transfers between devices with their start and end apart: 2 -> 14, of which waited for: 2 -> 11; matrix products, arithmetic and copies ran while one was open for 0% -> 0% of each run, Pallas kernels for 0% -> 3%
where the time goes in v1:
time: 46.3 us; the launch traced here: 46.1 us
  waiting for transfers between devices  19.2 us (41%)
  starting transfers between devices  17.3 us (37%)
  Pallas kernels  9.3 us (20%)
    ppermute x14, waiting for transfers between devices, exchange(): return lax.ppermute(value, axis, [(i, i ^ step) for i in range(size)])  19.2 us
    ppermute x14, starting transfers between devices, exchange(): return lax.ppermute(value, axis, [(i, i ^ step) for i in range(size)])  17.3 us
    pallas_call x1, Pallas kernels, first(): call(functools.partial(first_kernel, wide, chips), 'forward_first', (arra...  2.75 us
    pallas_call x1, Pallas kernels, backward_rest(): call(functools.partial(rest_kernel, wide), 'backward_rest', array(total.s...  2.37 us
    pallas_call x1, Pallas kernels, to_functions(): call(functools.partial(back_kernel, chips), 'functions_rest', tuple((arra...  1.07 us
  transfers between devices with their start and end apart: 14, of which 11 were waited for; matrix products, arithmetic and copies ran while one was open for 0% of the time, Pallas kernels for 3%

profile of v1, /device:TPU:0, one launch (start us, length us, event | category | flops | bytes accessed | tf_op | source)
XLA Modules:
  0.0 46.1 jit_solution(17311417000498325909)
XLA Ops:
  0.0 2.7 %forward_first.1 = (bf16[256,256]{1,0:T(8,128)(2,1)S(1)}, bf16[256,1024]{1,0:T(8,128)(2,1)S(1)}, bf16[1024,1024]{1,0:T(8,128)(2,1)S(1)}, bf16[4,256,2048]{2,1,0:T(8,128)(2,1)S(1)}, f32[32,2048]{1,0:T(8,128)S(1)}) custom-call(s32[16]{0:T(128)} %level_hbm.1, s32[16]{0:T(128)} %pad_ref.3, s32[16]{0:T(128)} %shift_hbm.1, bf16[1024,256]{1,0:T(8,128)(2,1)} %coeff_ref.1, ...), custom_call_target="tpu_custom_call" | custom-call | flops 134217728 | bytes 8388608 | tf_op jit(solution)/shard_map/forward_first/pallas_call | solution.py:119
  2.8 0.7 %forward_rest.1 = (f32[256,256]{1,0:T(8,128)S(1)}, bf16[256,256]{1,0:T(8,128)(2,1)S(1)}, bf16[256,256]{1,0:T(8,128)(2,1)S(1)}) custom-call(bf16[256,1024]{1,0:T(8,128)(2,1)S(1)} %get-tuple-element.24.turned_ref, bf16[1024,1024]{1,0:T(8,128)(2,1)S(1)} %get-tuple-element.23.rolled_ref), custom_call_target="tpu_custom_call" | custom-call | flops 402653184 | bytes 3145728 | tf_op jit(solution)/shard_map/forward_rest/pallas_call | solution.py:156
  3.5 3.0 %collective-permute-start = (bf16[256,256]{1,0:T(8,128)(2,1)S(1)}, bf16[256,256]{1,0:T(8,128)(2,1)S(1)}, u32[]{:S(2)}, u32[]{:S(2)}) collective-permute-start(bf16[256,256]{1,0:T(8,128)(2,1)S(1)} %get-tuple-element.26), channel_id=1, source_target_pairs={{0,8},{8,0},{16,24},{24,16},{1,9},{9,1},{17,25},{25,17},{2,10},{10... | collective-permute-start | bytes 393224 | tf_op jit(solution)/shard_map/ppermute | solution.py:392
  6.5 1.5 %collective-permute-start.1 = (bf16[256,256]{1,0:T(8,128)(2,1)S(1)}, bf16[256,256]{1,0:T(8,128)(2,1)S(1)}, u32[]{:S(2)}, u32[]{:S(2)}) collective-permute-start(bf16[256,256]{1,0:T(8,128)(2,1)S(1)} %get-tuple-element.27), channel_id=1, source_target_pairs={{0,16},{8,24},{16,0},{24,8},{1,17},{9,25},{17,1},{25,9},{2,18},{10... | collective-permute-start | bytes 393224 | tf_op jit(solution)/shard_map/ppermute | solution.py:392
  8.0 2.4 %collective-permute-done.refs_1_ = bf16[256,256]{1,0:T(8,128)(2,1)S(1)} collective-permute-done((bf16[256,256]{1,0:T(8,128)(2,1)S(1)}, bf16[256,256]{1,0:T(8,128)(2,1)S(1)}, u32[]{:S(2)}, u32[]{:S(2)}) %collective-permute-start) | collective-permute-done | bytes 131104 | tf_op jit(solution)/shard_map/ppermute | solution.py:392
  10.4 3.9 %collective-permute-done.1.refs_2_ = bf16[256,256]{1,0:T(8,128)(2,1)S(1)} collective-permute-done((bf16[256,256]{1,0:T(8,128)(2,1)S(1)}, bf16[256,256]{1,0:T(8,128)(2,1)S(1)}, u32[]{:S(2)}, u32[]{:S(2)}) %collective-permute-start.1) | collective-permute-done | bytes 131104 | tf_op jit(solution)/shard_map/ppermute | solution.py:392
  14.3 1.6 %collective-permute-start.3 = (bf16[64,256]{1,0:T(8,128)(2,1)S(1)}, bf16[64,256]{1,0:T(8,128)(2,1)S(1)}, u32[]{:S(2)}, u32[]{:S(2)}) collective-permute-start(bf16[64,256]{1,0:T(8,128)(2,1)S(1)} %get-tuple-element.31), channel_id=1, source_target_pairs={{0,2},{1,3},{2,0},{3,1},{4,6},{5,7},{6,4},{7,5},{8,10},{9,11},{10,... | collective-permute-start | bytes 98312 | tf_op jit(solution)/shard_map/ppermute | solution.py:392
  16.0 2.6 %collective-permute-start.4 = (bf16[64,256]{1,0:T(8,128)(2,1)S(1)}, bf16[64,256]{1,0:T(8,128)(2,1)S(1)}, u32[]{:S(2)}, u32[]{:S(2)}) collective-permute-start(bf16[64,256]{1,0:T(8,128)(2,1)S(1)} %get-tuple-element.32), channel_id=1, source_target_pairs={{0,4},{1,5},{2,6},{3,7},{4,0},{5,1},{6,2},{7,3},{8,12},{9,13},{10,... | collective-permute-start | bytes 98312 | tf_op jit(solution)/shard_map/ppermute | solution.py:392
  19.1 2.3 %collective-permute-done.4.refs_1_ = bf16[64,256]{1,0:T(8,128)(2,1)S(1)} collective-permute-done((bf16[64,256]{1,0:T(8,128)(2,1)S(1)}, bf16[64,256]{1,0:T(8,128)(2,1)S(1)}, u32[]{:S(2)}, u32[]{:S(2)}) %collective-permute-start.4) | collective-permute-done | bytes 32800 | tf_op jit(solution)/shard_map/ppermute | solution.py:392
  21.4 2.9 %collective-permute-done.5.refs_2_ = bf16[64,256]{1,0:T(8,128)(2,1)S(1)} collective-permute-done((bf16[64,256]{1,0:T(8,128)(2,1)S(1)}, bf16[64,256]{1,0:T(8,128)(2,1)S(1)}, u32[]{:S(2)}, u32[]{:S(2)}) %collective-permute-start.5) | collective-permute-done | bytes 32800 | tf_op jit(solution)/shard_map/ppermute | solution.py:392
  24.3 0.7 %points_rest.1 = (f32[32,2048]{1,0:T(8,128)S(1)}, f32[32,2048]{1,0:T(8,128)S(1)}) custom-call(f32[64,2048]{1,0:T(8,128)S(1)} %points_own.1.total_ref, bf16[64,256]{1,0:T(8,128)(2,1)S(1)} %collective-permute-done.3.refs_0_, bf16[64,256]{1,0:T(8,128)(2,1)S(1)} %collective-permute-done.4.refs_1_, bf16[64,256]{1,0:T(8,128)(2,1)S(1)} %collective-permute-done.5.refs_2_, ...), custom_call_target="tpu_custom_call" | custom-call | flops 201326592 | bytes 4194304 | tf_op jit(solution)/shard_map/points_rest/pallas_call | solution.py:231
  25.0 1.5 %collective-permute-done.6.other_ref = f32[32,2048]{1,0:T(8,128)S(1)} collective-permute-done((f32[32,2048]{1,0:T(8,128)S(1)}, f32[32,2048]{1,0:T(8,128)S(1)}, u32[]{:S(2)}, u32[]{:S(2)}) %collective-permute-start.6) | collective-permute-done | bytes 262176 | tf_op jit(solution)/shard_map/ppermute | solution.py:392
  26.9 1.2 %collective-permute-done.7.other_ref = bf16[32,2048]{1,0:T(8,128)(2,1)S(1)} collective-permute-done((bf16[32,2048]{1,0:T(8,128)(2,1)S(1)}, bf16[32,2048]{1,0:T(8,128)(2,1)S(1)}, u32[]{:S(2)}, u32[]{:S(2)}) %collective-permute-start.7) | collective-permute-done | bytes 131104 | tf_op jit(solution)/shard_map/ppermute | solution.py:392
  28.1 1.1 %functions_rest.1 = (bf16[64,256]{1,0:T(8,128)(2,1)S(1)}, bf16[64,256]{1,0:T(8,128)(2,1)S(1)}, bf16[64,256]{1,0:T(8,128)(2,1)S(1)}, bf16[64,2048]{1,0:T(8,128)(2,1)S(1)}) custom-call(bf16[32,2048]{1,0:T(8,128)(2,1)S(1)} %act.1.mine_ref, bf16[32,2048]{1,0:T(8,128)(2,1)S(1)} %collective-permute-done.7.other_ref, ...), custom_call_target="tpu_custom_call" | custom-call | flops 201326592 | bytes 4194304 | tf_op jit(solution)/shard_map/functions_rest/pallas_call | solution.py:268
  29.6 4.0 %collective-permute-start.9 = (bf16[64,256]{1,0:T(8,128)(2,1)S(1)}, bf16[64,256]{1,0:T(8,128)(2,1)S(1)}, u32[]{:S(2)}, u32[]{:S(2)}) collective-permute-start(bf16[64,256]{1,0:T(8,128)(2,1)S(1)} %get-tuple-element.39), channel_id=1, source_target_pairs={{0,4},{1,5},{2,6},{3,7},{4,0},{5,1},{6,2},{7,3},{8,12},{9,13},{10,... | collective-permute-start | bytes 98312 | tf_op jit(solution)/shard_map/ppermute | solution.py:392
  33.6 0.4 functions_own.1.refs_0_
  34.0 1.1 %collective-permute-done.10.refs_3_ = bf16[64,256]{1,0:T(8,128)(2,1)S(1)} collective-permute-done((bf16[64,256]{1,0:T(8,128)(2,1)S(1)}, bf16[64,256]{1,0:T(8,128)(2,1)S(1)}, u32[]{:S(2)}, u32[]{:S(2)}) %collective-permute-start.10) | collective-permute-done | bytes 32800 | tf_op jit(solution)/shard_map/ppermute | solution.py:392
  35.5 1.3 %collective-permute-start.11 = (bf16[256,256]{1,0:T(8,128)(2,1)S(1)}, bf16[256,256]{1,0:T(8,128)(2,1)S(1)}, u32[]{:S(2)}, u32[]{:S(2)}) collective-permute-start(bf16[256,256]{1,0:T(8,128)(2,1)S(1)} %assemble.1.grid_ref), channel_id=1, source_target_pairs={{0,8},{8,0},{16,24},{24,16},{1,9},{9,1},{17,25},{25,17},{2,10},{10... | collective-permute-start | bytes 393224 | tf_op jit(solution)/shard_map/ppermute | solution.py:392
  36.8 0.8 %collective-permute-start.12 = (bf16[256,256]{1,0:T(8,128)(2,1)S(1)}, bf16[256,256]{1,0:T(8,128)(2,1)S(1)}, u32[]{:S(2)}, u32[]{:S(2)}) collective-permute-start(bf16[256,256]{1,0:T(8,128)(2,1)S(1)} %assemble.1.grid_ref), channel_id=1, source_target_pairs={{0,16},{8,24},{16,0},{24,8},{1,17},{9,25},{17,1},{25,9},{2,18},{10... | collective-permute-start | bytes 393224 | tf_op jit(solution)/shard_map/ppermute | solution.py:392
  37.6 1.4 %collective-permute-start.13 = (bf16[256,256]{1,0:T(8,128)(2,1)S(1)}, bf16[256,256]{1,0:T(8,128)(2,1)}, u32[]{:S(2)}, u32[]{:S(2)}) collective-permute-start(bf16[256,256]{1,0:T(8,128)(2,1)S(1)} %assemble.1.grid_ref), channel_id=1, source_target_pairs={{0,24},{8,16},{16,8},{24,0},{1,25},{9,17},{17,9},{25,1},{2,26},{10... | collective-permute-start | bytes 393224 | tf_op jit(solution)/shard_map/ppermute | solution.py:392
  39.3 0.8 %backward_own.1.total_ref = f32[1024,256]{1,0:T(8,128)S(1)} custom-call(s32[16]{0:T(128)S(1)} %copy-done.1, bf16[1024,1024]{1,0:T(8,128)(2,1)S(1)} %get-tuple-element.23.rolled_ref, bf16[256,256]{1,0:T(8,128)(2,1)S(1)} %assemble.1.grid_ref, bf16[1024,256]{1,0:T(8,128)(2,1)S(1)} %copy-done, f32[1024,1]{1,0:T(8,128)S(1)} %copy.10.row_ref, f32[1,256]{1,0:T(1,128)S(1)} %bitcast.3), custom_call_target="tpu_custom_call" | custom-call | flops 134217728 | bytes 4194304 | tf_op jit(solution)/shard_map/backward_own/pallas_call | solution.py:337
  40.2 1.7 %collective-permute-done.11.refs_0_ = bf16[256,256]{1,0:T(8,128)(2,1)S(1)} collective-permute-done((bf16[256,256]{1,0:T(8,128)(2,1)S(1)}, bf16[256,256]{1,0:T(8,128)(2,1)S(1)}, u32[]{:S(2)}, u32[]{:S(2)}) %collective-permute-start.11) | collective-permute-done | bytes 131104 | tf_op jit(solution)/shard_map/ppermute | solution.py:392
  41.9 1.8 %collective-permute-done.12.refs_1_ = bf16[256,256]{1,0:T(8,128)(2,1)S(1)} collective-permute-done((bf16[256,256]{1,0:T(8,128)(2,1)S(1)}, bf16[256,256]{1,0:T(8,128)(2,1)S(1)}, u32[]{:S(2)}, u32[]{:S(2)}) %collective-permute-start.12) | collective-permute-done | bytes 131104 | tf_op jit(solution)/shard_map/ppermute | solution.py:392
  43.8 2.4 %backward_rest.1 = f32[1024,256]{1,0:T(8,128)} custom-call(s32[16]{0:T(128)S(1)} %copy-done.1, f32[1024,256]{1,0:T(8,128)S(1)} %backward_own.1.total_ref, bf16[1024,1024]{1,0:T(8,128)(2,1)S(1)} %get-tuple-element.23.rolled_ref, bf16[256,256]{1,0:T(8,128)(2,1)S(1)} %collective-permute-done.11.refs_0_, bf16[256,256]{1,0:T(8,128)(2,1)S(1)} %collective-permute-done.12.refs_1_, ...), custom_call_target="tpu_custom_call" | custom-call | flops 536870912 | bytes 4194304 | tf_op jit(solution)/shard_map/backward_rest/pallas_call | solution.py:379
  (24 shorter events, 2.0 us)
Async XLA Ops:
  3.5 6.9 %collective-permute-start = (bf16[256,256]{1,0:T(8,128)(2,1)S(1)}, bf16[256,256]{1,0:T(8,128)(2,1)S(1)}, u32[]{:S(2)}, u32[]{:S(2)}) collective-permute-start(bf16[256,256]{1,0:T(8,128)(2,1)S(1)} %get-tuple-element.26), channel_id=1, source_target_pairs={{0,8},{8,0},{16,24},{24,16},{1,9},{9,1},{17,25},{25,17},{2,10},{10... | collective-permute-start | bytes 393224 | tf_op jit(solution)/shard_map/ppermute | solution.py:392
  6.5 7.8 %collective-permute-start.1 = (bf16[256,256]{1,0:T(8,128)(2,1)S(1)}, bf16[256,256]{1,0:T(8,128)(2,1)S(1)}, u32[]{:S(2)}, u32[]{:S(2)}) collective-permute-start(bf16[256,256]{1,0:T(8,128)(2,1)S(1)} %get-tuple-element.27), channel_id=1, source_target_pairs={{0,16},{8,24},{16,0},{24,8},{1,17},{9,25},{17,1},{25,9},{2,18},{10... | collective-permute-start | bytes 393224 | tf_op jit(solution)/shard_map/ppermute | solution.py:392
  8.0 6.3 %collective-permute-start.2 = (bf16[256,256]{1,0:T(8,128)(2,1)S(1)}, bf16[256,256]{1,0:T(8,128)(2,1)S(1)}, u32[]{:S(2)}, u32[]{:S(2)}) collective-permute-start(bf16[256,256]{1,0:T(8,128)(2,1)S(1)} %get-tuple-element.28), channel_id=1, source_target_pairs={{0,24},{8,16},{16,8},{24,0},{1,25},{9,17},{17,9},{25,1},{2,26},{10... | collective-permute-start | bytes 393224 | tf_op jit(solution)/shard_map/ppermute | solution.py:392
  14.3 4.8 %collective-permute-start.3 = (bf16[64,256]{1,0:T(8,128)(2,1)S(1)}, bf16[64,256]{1,0:T(8,128)(2,1)S(1)}, u32[]{:S(2)}, u32[]{:S(2)}) collective-permute-start(bf16[64,256]{1,0:T(8,128)(2,1)S(1)} %get-tuple-element.31), channel_id=1, source_target_pairs={{0,2},{1,3},{2,0},{3,1},{4,6},{5,7},{6,4},{7,5},{8,10},{9,11},{10,... | collective-permute-start | bytes 98312 | tf_op jit(solution)/shard_map/ppermute | solution.py:392
  16.0 5.4 %collective-permute-start.4 = (bf16[64,256]{1,0:T(8,128)(2,1)S(1)}, bf16[64,256]{1,0:T(8,128)(2,1)S(1)}, u32[]{:S(2)}, u32[]{:S(2)}) collective-permute-start(bf16[64,256]{1,0:T(8,128)(2,1)S(1)} %get-tuple-element.32), channel_id=1, source_target_pairs={{0,4},{1,5},{2,6},{3,7},{4,0},{5,1},{6,2},{7,3},{8,12},{9,13},{10,... | collective-permute-start | bytes 98312 | tf_op jit(solution)/shard_map/ppermute | solution.py:392
  18.5 5.7 %collective-permute-start.5 = (bf16[64,256]{1,0:T(8,128)(2,1)S(1)}, bf16[64,256]{1,0:T(8,128)(2,1)S(1)}, u32[]{:S(2)}, u32[]{:S(2)}) collective-permute-start(bf16[64,256]{1,0:T(8,128)(2,1)S(1)} %get-tuple-element.33), channel_id=1, source_target_pairs={{0,6},{1,7},{2,4},{3,5},{4,2},{5,3},{6,0},{7,1},{8,14},{9,15},{10,... | collective-permute-start | bytes 98312 | tf_op jit(solution)/shard_map/ppermute | solution.py:392
  25.0 1.6 %collective-permute-start.6 = (f32[32,2048]{1,0:T(8,128)S(1)}, f32[32,2048]{1,0:T(8,128)S(1)}, u32[]{:S(2)}, u32[]{:S(2)}) collective-permute-start(f32[32,2048]{1,0:T(8,128)S(1)} %get-tuple-element.35), channel_id=1, source_target_pairs={{0,1},{1,0},{2,3},{3,2},{4,5},{5,4},{6,7},{7,6},{8,9},{9,8},{10,11... | collective-permute-start | bytes 786440 | tf_op jit(solution)/shard_map/ppermute | solution.py:392
  26.6 12.5 %copy-start.3 = (f32[1024]{0:T(1024)S(1)}, f32[1024]{0:T(1024)}, u32[]{:S(2)}) copy-start(f32[1024]{0:T(1024)} %param.10) | copy-start | bytes 12292
  26.6 12.7 %copy-start = (bf16[1024,256]{1,0:T(8,128)(2,1)S(1)}, bf16[1024,256]{1,0:T(8,128)(2,1)}, u32[]{:S(2)}) copy-start(bf16[1024,256]{1,0:T(8,128)(2,1)} %coeff_ref.1) | copy-start | bytes 1572868
  26.6 12.7 %copy-start.1 = (s32[16]{0:T(128)S(1)}, s32[16]{0:T(128)}, u32[]{:S(2)}) copy-start(s32[16]{0:T(128)} %pad_ref.3) | copy-start | bytes 196
  26.6 12.7 %copy-start.2 = (f32[256]{0:T(256)S(1)}, f32[256]{0:T(256)}, u32[]{:S(2)}) copy-start(f32[256]{0:T(256)} %param.11) | copy-start | bytes 3076
  26.7 1.4 %collective-permute-start.7 = (bf16[32,2048]{1,0:T(8,128)(2,1)S(1)}, bf16[32,2048]{1,0:T(8,128)(2,1)S(1)}, u32[]{:S(2)}, u32[]{:S(2)}) collective-permute-start(bf16[32,2048]{1,0:T(8,128)(2,1)S(1)} %act.1.mine_ref), channel_id=1, source_target_pairs={{0,1},{1,0},{2,3},{3,2},{4,5},{5,4},{6,7},{7,6},{8,9},{9,8},{10,11... | collective-permute-start | bytes 393224 | tf_op jit(solution)/shard_map/ppermute | solution.py:392
  29.1 6.0 %collective-permute-start.10 = (bf16[64,256]{1,0:T(8,128)(2,1)S(1)}, bf16[64,256]{1,0:T(8,128)(2,1)S(1)}, u32[]{:S(2)}, u32[]{:S(2)}) collective-permute-start(bf16[64,256]{1,0:T(8,128)(2,1)S(1)} %get-tuple-element.40), channel_id=1, source_target_pairs={{0,6},{1,7},{2,4},{3,5},{4,2},{5,3},{6,0},{7,1},{8,14},{9,15},{10,... | collective-permute-start | bytes 98312 | tf_op jit(solution)/shard_map/ppermute | solution.py:392
  29.6 5.6 %collective-permute-start.8 = (bf16[64,256]{1,0:T(8,128)(2,1)S(1)}, bf16[64,256]{1,0:T(8,128)(2,1)S(1)}, u32[]{:S(2)}, u32[]{:S(2)}) collective-permute-start(bf16[64,256]{1,0:T(8,128)(2,1)S(1)} %get-tuple-element.38), channel_id=1, source_target_pairs={{0,2},{1,3},{2,0},{3,1},{4,6},{5,7},{6,4},{7,5},{8,10},{9,11},{10,... | collective-permute-start | bytes 98312 | tf_op jit(solution)/shard_map/ppermute | solution.py:392
  29.6 5.9 %collective-permute-start.9 = (bf16[64,256]{1,0:T(8,128)(2,1)S(1)}, bf16[64,256]{1,0:T(8,128)(2,1)S(1)}, u32[]{:S(2)}, u32[]{:S(2)}) collective-permute-start(bf16[64,256]{1,0:T(8,128)(2,1)S(1)} %get-tuple-element.39), channel_id=1, source_target_pairs={{0,4},{1,5},{2,6},{3,7},{4,0},{5,1},{6,2},{7,3},{8,12},{9,13},{10,... | collective-permute-start | bytes 98312 | tf_op jit(solution)/shard_map/ppermute | solution.py:392
  35.5 6.4 %collective-permute-start.11 = (bf16[256,256]{1,0:T(8,128)(2,1)S(1)}, bf16[256,256]{1,0:T(8,128)(2,1)S(1)}, u32[]{:S(2)}, u32[]{:S(2)}) collective-permute-start(bf16[256,256]{1,0:T(8,128)(2,1)S(1)} %assemble.1.grid_ref), channel_id=1, source_target_pairs={{0,8},{8,0},{16,24},{24,16},{1,9},{9,1},{17,25},{25,17},{2,10},{10... | collective-permute-start | bytes 393224 | tf_op jit(solution)/shard_map/ppermute | solution.py:392
  36.8 6.9 %collective-permute-start.12 = (bf16[256,256]{1,0:T(8,128)(2,1)S(1)}, bf16[256,256]{1,0:T(8,128)(2,1)S(1)}, u32[]{:S(2)}, u32[]{:S(2)}) collective-permute-start(bf16[256,256]{1,0:T(8,128)(2,1)S(1)} %assemble.1.grid_ref), channel_id=1, source_target_pairs={{0,16},{8,24},{16,0},{24,8},{1,17},{9,25},{17,1},{25,9},{2,18},{10... | collective-permute-start | bytes 393224 | tf_op jit(solution)/shard_map/ppermute | solution.py:392
  37.6 6.1 %collective-permute-start.13 = (bf16[256,256]{1,0:T(8,128)(2,1)S(1)}, bf16[256,256]{1,0:T(8,128)(2,1)}, u32[]{:S(2)}, u32[]{:S(2)}) collective-permute-start(bf16[256,256]{1,0:T(8,128)(2,1)S(1)} %assemble.1.grid_ref), channel_id=1, source_target_pairs={{0,24},{8,16},{16,8},{24,0},{1,25},{9,17},{17,9},{25,1},{2,26},{10... | collective-permute-start | bytes 393224 | tf_op jit(solution)/shard_map/ppermute | solution.py:392

commit v2 on v1

--- a/solution.py
+++ b/solution.py
@@ -54,7 +54,6 @@
     basis_hbm,
     potential_hbm,
     out_ref,
-    turned_ref,
     rolled_ref,
     basis_ref,
     potential_ref,
@@ -63,10 +62,11 @@
     shift_ref,
     coeff_ref,
     table_ref,
+    turned_ref,
     sems,
 ):
     place = lax.axis_index("narrow")
-    core, chip = place % 2, place // 2
+    core = place % 2
     columns = coeff_ref.shape[1]
     pairs = [
         (level_hbm, level_ref),
@@ -77,7 +77,7 @@
         (potential_hbm, potential_ref),
     ]
     for j in range(chips):
-        start = pl.multiple_of(((chip ^ j) * 2 + core) * columns, columns)
+        start = pl.multiple_of((j * 2 + core) * columns, columns)
         pairs.append((basis_hbm.at[pl.ds(start, columns), :], basis_ref.at[j]))
     copies = [
         pltpu.make_async_copy(source, target, sems.at[i])
@@ -101,11 +101,10 @@
         piece = coeff_ref[rows, :].astype(F32)
         pieces.append(jnp.where(row < width - pad_ref[s], piece, 0.0))
     turned_ref[...] = jnp.concatenate(pieces, axis=0).T.astype(BF16)
-    me = lax.axis_index("wide")
     own = rolled_ref.shape[1] // wide
-    start = pl.multiple_of((me ^ (wide - 1)) * own, own)
-    total = dot(turned_ref[...], rolled_ref[:, pl.ds(start, own)])
-    out_ref[...] = total.T.astype(BF16)
+    for d in range(wide):
+        total = dot(turned_ref[...], rolled_ref[:, d * own : (d + 1) * own])
+        out_ref[d] = total.T.astype(BF16)
     for copy in copies[5:]:
         copy.wait()
 
@@ -120,20 +119,20 @@
         functools.partial(first_kernel, wide, chips),
         "forward_first",
         (
-            array((own, columns), BF16),
-            array((columns, rows), BF16),
+            array((wide, own, columns), BF16),
             array((rows, points), BF16),
             array((chips, columns, basis.shape[1]), BF16),
             array(potential.shape, F32),
         ),
         [HBM] * 7,
-        (VMEM,) * 5,
+        (VMEM,) * 4,
         [
             pltpu.SMEM((slots,), jnp.int32),
             pltpu.SMEM((slots,), jnp.int32),
             pltpu.SMEM((slots,), jnp.int32),
             pltpu.VMEM(coeff.shape, coeff.dtype),
             pltpu.VMEM(tables.shape, tables.dtype),
+            pltpu.VMEM((columns, rows), BF16),
             pltpu.SemaphoreType.DMA((6 + chips,)),
         ],
         flops=2 * rows * own * columns,
@@ -141,103 +140,35 @@
     )(*(in_hbm(value) for value in inputs))
 
 
-def second_kernel(wide, turned_ref, rolled_ref, *outs):
-    me = lax.axis_index("wide")
-    own = rolled_ref.shape[1] // wide
-    for k in range(wide - 1):
-        start = pl.multiple_of((me ^ k) * own, own)
-        total = dot(turned_ref[...], rolled_ref[:, pl.ds(start, own)])
-        outs[k][...] = total.T.astype(outs[k].dtype)
-
-
-def second(wide, turned, rolled):
-    columns, rows = turned.shape
-    own = rolled.shape[1] // wide
-    return call(
-        functools.partial(second_kernel, wide),
-        "forward_rest",
-        tuple(array((own, columns), BF16 if k else F32) for k in range(wide - 1)),
-        [VMEM] * 2,
-        (VMEM,) * (wide - 1),
-        flops=2 * rows * own * columns * (wide - 1),
-        moved=3 * MIB,
-    )(turned, rolled)
-
-
-def combine_kernel(wide, chips, *refs):
-    parts, outs = refs[:wide], refs[wide:]
-    chip = lax.axis_index("narrow") // 2
-    rows = outs[0].shape[0]
-    for j in range(chips):
-        start = pl.multiple_of((chip ^ j) * rows, rows)
-        total = parts[0][pl.ds(start, rows), :]
-        for part in parts[1:]:
-            total = total + part[pl.ds(start, rows), :].astype(F32)
-        outs[j][...] = total.astype(BF16)
-
-
-def combine(chips, parts):
-    rows, columns = parts[0].shape
-    wide = len(parts)
-    return call(
-        functools.partial(combine_kernel, wide, chips),
-        "wide_sum",
-        tuple(array((rows // chips, columns), BF16) for _ in range(chips)),
-        [VMEM] * wide,
-        (VMEM,) * chips,
-        moved=MIB,
-    )(*parts)
-
-
-def early_kernel(x_ref, basis_ref, out_ref):
-    out_ref[...] = dot(x_ref[...], basis_ref[0])
-
-
-def early(x, basis):
-    rows = x.shape[0]
-    points = basis.shape[2]
-    return call(
-        early_kernel,
-        "points_own",
-        array((rows, points), F32),
-        [VMEM] * 2,
-        VMEM,
-        flops=2 * rows * points * x.shape[1],
-        moved=2 * MIB,
-    )(x, basis)
-
-
-def points_kernel(chips, total_ref, *refs):
-    xs = refs[: chips - 1]
-    basis_ref, mine_ref, theirs_ref, sum_ref = refs[chips - 1 :]
+def points_kernel(x_ref, basis_ref, mine_ref, theirs_ref, sum_ref):
     core = lax.axis_index("narrow") % 2
-    rows = mine_ref.shape[0]
-    points = mine_ref.shape[1]
+    chips = x_ref.shape[0]
+    rows, points = mine_ref.shape
     step = min(points, 512)
     for p in range(0, points, step):
         span = slice(p, p + step)
-        total = total_ref[:, span]
+        total = dot(x_ref[0], basis_ref[0, :, span])
         for j in range(1, chips):
-            total = total + dot(xs[j - 1][...], basis_ref[j, :, span])
+            total = total + dot(x_ref[j], basis_ref[j, :, span])
         sum_ref[:, span] = total
     mine_ref[...] = sum_ref[pl.ds(pl.multiple_of(core * rows, rows), rows), :]
     theirs_ref[...] = sum_ref[pl.ds(pl.multiple_of((1 - core) * rows, rows), rows), :]
 
 
-def to_points(total, xs, basis):
-    rows, points = total.shape
+def to_points(x, basis):
+    chips, rows, columns = x.shape
+    points = basis.shape[2]
     half = array((rows // 2, points), F32)
-    chips = len(xs) + 1
-    return call(
-        functools.partial(points_kernel, chips),
-        "points_rest",
+    return call(
+        points_kernel,
+        "points",
         (half, half),
-        [VMEM] * (chips + 1),
+        [VMEM] * 2,
         (VMEM, VMEM),
         [pltpu.VMEM((rows, points), F32)],
-        flops=2 * rows * points * xs[0].shape[1] * (chips - 1),
+        flops=2 * rows * points * columns * chips,
         moved=4 * MIB,
-    )(total, *xs, basis)
+    )(x, basis)
 
 
 def act_kernel(mine_ref, other_ref, potential_ref, out_ref):
@@ -251,71 +182,29 @@
     )(mine, other, potential)
 
 
-def back_kernel(chips, mine_ref, other_ref, basis_ref, *refs):
-    outs, both_ref, rows_ref = refs[:chips - 1], refs[chips - 1], refs[chips]
+def back_kernel(mine_ref, other_ref, basis_ref, out_ref, rows_ref):
     core = lax.axis_index("narrow") % 2
     rows = mine_ref.shape[0]
     rows_ref[pl.ds(pl.multiple_of(core * rows, rows), rows), :] = mine_ref[...].astype(F32)
     rows_ref[pl.ds(pl.multiple_of((1 - core) * rows, rows), rows), :] = other_ref[...].astype(F32)
-    both_ref[...] = rows_ref[...].astype(BF16)
-    for j in range(1, chips):
-        outs[j - 1][...] = dot_turned(both_ref[...], basis_ref[j]).astype(BF16)
+    both = rows_ref[...].astype(BF16)
+    for j in range(out_ref.shape[0]):
+        out_ref[j] = dot_turned(both, basis_ref[j]).astype(BF16)
 
 
 def to_functions(mine, other, basis):
     rows, points = mine.shape
     chips, columns, _ = basis.shape
     return call(
-        functools.partial(back_kernel, chips),
-        "functions_rest",
-        tuple(array((2 * rows, columns), BF16) for _ in range(chips - 1))
-        + (array((2 * rows, points), BF16),),
+        back_kernel,
+        "functions",
+        array((chips, 2 * rows, columns), BF16),
         [VMEM] * 3,
-        (VMEM,) * chips,
+        VMEM,
         [pltpu.VMEM((2 * rows, points), F32)],
-        flops=4 * rows * points * columns * (chips - 1),
+        flops=4 * rows * points * columns * chips,
         moved=4 * MIB,
     )(mine, other, basis)
-
-
-def late_kernel(both_ref, basis_ref, out_ref):
-    out_ref[...] = dot_turned(both_ref[...], basis_ref[0]).astype(BF16)
-
-
-def late(both, basis):
-    rows, points = both.shape
-    columns = basis.shape[1]
-    return call(
-        late_kernel,
-        "functions_own",
-        array((rows, columns), BF16),
-        [VMEM] * 2,
-        VMEM,
-        flops=2 * rows * points * columns,
-        moved=2 * MIB,
-    )(both, basis)
-
-
-def assemble_kernel(*refs):
-    parts, out_ref = refs[:-1], refs[-1]
-    chip = lax.axis_index("narrow") // 2
-    rows = parts[0].shape[0]
-    for j, part in enumerate(parts):
-        start = pl.multiple_of((chip ^ j) * rows, rows)
-        out_ref[pl.ds(start, rows), :] = part[...]
-
-
-def assemble(parts):
-    rows, columns = parts[0].shape
-    chips = len(parts)
-    return call(
-        assemble_kernel,
-        "assemble",
-        array((rows * chips, columns), BF16),
-        [VMEM] * chips,
-        VMEM,
-        moved=MIB // 4,
-    )(*parts)
 
 
 def own_kernel(wide, pad_ref, rolled_ref, grid_ref, coeff_ref, row_ref, column_ref, out_ref):
@@ -392,6 +281,13 @@
     return lax.ppermute(value, axis, [(i, i ^ step) for i in range(size)])
 
 
+def along_z(value, narrow):
+    groups = [list(range(core, narrow, 2)) for core in range(2)]
+    return lax.all_to_all(
+        value, "narrow", split_axis=0, concat_axis=0, axis_index_groups=groups, tiled=True
+    )
+
+
 def body(
     wide,
     narrow,
@@ -407,7 +303,7 @@
 ):
     chips = narrow // 2
     tables = jnp.swapaxes(groupb_basis_values, 1, 2)
-    far, turned, rolled, basis, pot = first(
+    parts, rolled, basis, pot = first(
         wide,
         chips,
         slot_sparse_level,
@@ -418,19 +314,15 @@
         basis_a,
         potential,
     )
-    arrived = {wide - 1: exchange(far, wide - 1, wide, "wide")}
-    parts = second(wide, turned, rolled)
-    for k in range(1, wide - 1):
-        arrived[k] = exchange(parts[k], k, wide, "wide")
-    pieces = combine(chips, [parts[0]] + [arrived[k] for k in range(1, wide)])
-    xs = [exchange(pieces[j], 2 * j, narrow, "narrow") for j in range(1, chips)]
-    total = early(pieces[0], basis)
-    mine, theirs = to_points(total, xs, basis)
+    columns = coeff.shape[1]
+    arrived = lax.all_to_all(parts, "wide", split_axis=0, concat_axis=0, tiled=True)
+    summed = jnp.sum(arrived.astype(F32), axis=0).astype(BF16)
+    x = along_z(summed.reshape(chips, summed.shape[0] // chips, columns), narrow)
+    mine, theirs = to_points(x, basis)
     acted = act(mine, exchange(theirs, 1, narrow, "narrow"), pot)
     other = exchange(acted, 1, narrow, "narrow")
-    *blocks, both = to_functions(acted, other, basis)
-    sent = [exchange(blocks[j - 1], 2 * j, narrow, "narrow") for j in range(1, chips)]
-    grid = assemble([late(both, basis)] + sent)
+    blocks = along_z(to_functions(acted, other, basis), narrow)
+    grid = blocks.reshape(summed.shape)
     grids = [exchange(grid, k, wide, "wide") for k in range(1, wide)]
     start = backward_own(
         wide, block_pad, rolled, grid, coeff, groupb_row_energy, groupa_energy

time: 46.3 us -> 55.8 us (1.21)
  blocking collectives: 0 us -> 33 us
  waiting for transfers between devices: 19.2 us -> 5.63 us
  starting transfers between devices: 17.3 us -> 3.76 us
  local copies, waits for them, and re-layouts: 0.24 us -> 4.38 us
  Pallas kernels: 9.3 us -> 8.64 us
    all_to_all x0 -> x3, blocking collectives: none -> 33 us  [the longest x2 19.5 us: along_z(): lax.all_to_all(value, 'narrow', split_axis=0, concat_axis=0, axis_index_g...]
    ppermute x14 -> x5, waiting for transfers between devices: 19.2 us -> 5.63 us  [exchange(): return lax.ppermute(value, axis, [(i, i ^ step) for i in range(size)])]
    ppermute x14 -> x5, starting transfers between devices: 17.3 us -> 3.76 us  [exchange(): return lax.ppermute(value, axis, [(i, i ^ step) for i in range(size)])]
    unnamed x8 -> x14, local copies, waits for them, and re-layouts: 0.03 us -> 4.16 us
    pallas_call x7 -> x2, Pallas kernels: 3.29 us -> 2.25 us  [the longest x1 1.38 us: to_functions(): call(back_kernel, 'functions', array((chips, 2 * rows, columns), BF16), [...]
  transfers between devices with their start and end apart: 14 -> 5, of which waited for: 11 -> 5; matrix products, arithmetic and copies ran while one was open for 0% -> 0% of each run, Pallas kernels for 3% -> 2%
where the time goes in v2:
time: 55.8 us; the launch traced here: 55.6 us
  blocking collectives  33 us (59%)
  Pallas kernels  8.64 us (15%)
  waiting for transfers between devices  5.63 us (10%)
  local copies, waits for them, and re-layouts  4.38 us (8%)
  starting transfers between devices  3.76 us (7%)
    all_to_all x2, blocking collectives, along_z(): lax.all_to_all(value, 'narrow', split_axis=0, concat_axis=0, axis_index_g...  19.5 us
    all_to_all x1, blocking collectives, body(): lax.all_to_all(parts, 'wide', split_axis=0, concat_axis=0, tiled=True)  13.5 us
    ppermute x5, waiting for transfers between devices, exchange(): return lax.ppermute(value, axis, [(i, i ^ step) for i in range(size)])  5.63 us
    unnamed x14, local copies, waits for them, and re-layouts  4.16 us
    ppermute x5, starting transfers between devices, exchange(): return lax.ppermute(value, axis, [(i, i ^ step) for i in range(size)])  3.76 us
    pallas_call x1, Pallas kernels, first(): call(functools.partial(first_kernel, wide, chips), 'forward_first', (arra...  3.14 us
    pallas_call x1, Pallas kernels, backward_rest(): call(functools.partial(rest_kernel, wide), 'backward_rest', array(total.s...  2.37 us
    pallas_call x1, Pallas kernels, to_functions(): call(back_kernel, 'functions', array((chips, 2 * rows, columns), BF16), [...  1.38 us
  transfers between devices with their start and end apart: 5, of which 5 were waited for; matrix products, arithmetic and copies ran while one was open for 0% of the time, Pallas kernels for 2%

profile of v2, /device:TPU:0, one launch (start us, length us, event | category | flops | bytes accessed | tf_op | source)
XLA Modules:
  0.0 55.6 jit_solution(14327304063630712517)
XLA Ops:
  0.0 3.1 %forward_first.1 = (bf16[4,256,256]{2,1,0:T(8,128)(2,1)S(1)}, bf16[1024,1024]{1,0:T(8,128)(2,1)S(1)}, bf16[4,256,2048]{2,1,0:T(8,128)(2,1)S(1)}, f32[32,2048]{1,0:T(8,128)S(1)}) custom-call(s32[16]{0:T(128)} %level_hbm.1, s32[16]{0:T(128)} %pad_ref.3, s32[16]{0:T(128)} %shift_hbm.1, bf16[1024,256]{1,0:T(8,128)(2,1)} %coeff_ref.1, ...), custom_call_target="tpu_custom_call" | custom-call | flops 134217728 | bytes 8388608 | tf_op jit(solution)/shard_map/forward_first/pallas_call | solution.py:118
  3.2 1.9 %copy-done = bf16[4,256,2048]{2,1,0:T(8,128)(2,1)} copy-done((bf16[4,256,2048]{2,1,0:T(8,128)(2,1)}, bf16[4,256,2048]{2,1,0:T(8,128)(2,1)S(1)}, u32[]{:S(2)}) %copy-start) | copy-done | bytes 4194328
  5.1 13.5 %all_to_all.15 = bf16[4,256,256]{2,1,0:T(8,128)(2,1)S(1)} all-to-all(bf16[4,256,256]{2,1,0:T(8,128)(2,1)S(1)} %get-tuple-element.12), channel_id=1, replica_groups=mesh['wide'=4,'narrow'=8] {'wide'}, dimensions={0} | all-to-all | bytes 1048576 | tf_op jit(solution)/shard_map/all_to_all | solution.py:318
  18.6 0.1 reduce_sum.12
  18.7 10.6 %all_to_all.16.x_ref = bf16[4,64,256]{2,1,0:T(8,128)(2,1)S(1)} all-to-all(bf16[4,64,256]{2,1,0:T(8,128)(2,1)S(1)} %bitcast.11), channel_id=1, replica_groups={{0,2,4,6},{1,3,5,7},{8,10,12,14},{9,11,13,15},{16,18,20,22},{17,19,21,2..., dimensions={0} | all-to-all | bytes 262144 | tf_op jit(solution)/shard_map/all_to_all | solution.py:286
  29.2 2.2 %copy-done.1 = bf16[4,256,2048]{2,1,0:T(8,128)(2,1)S(1)} copy-done((bf16[4,256,2048]{2,1,0:T(8,128)(2,1)S(1)}, bf16[4,256,2048]{2,1,0:T(8,128)(2,1)}, u32[]{:S(2)}) %copy-start.1) | copy-done | bytes 4194328
  31.4 0.9 %points.1 = (f32[32,2048]{1,0:T(8,128)S(1)}, f32[32,2048]{1,0:T(8,128)S(1)}) custom-call(bf16[4,64,256]{2,1,0:T(8,128)(2,1)S(1)} %all_to_all.16.x_ref, bf16[4,256,2048]{2,1,0:T(8,128)(2,1)S(1)} %copy-done.1), custom_call_target="tpu_custom_call" | custom-call | flops 268435456 | bytes 4194304 | tf_op jit(solution)/shard_map/points/pallas_call | solution.py:162
  32.3 0.0 copy-start.3
  32.3 0.0 copy-start.4
  32.3 0.1 collective-permute-start
  32.4 1.5 %collective-permute-done.other_ref = f32[32,2048]{1,0:T(8,128)S(1)} collective-permute-done((f32[32,2048]{1,0:T(8,128)S(1)}, f32[32,2048]{1,0:T(8,128)S(1)}, u32[]{:S(2)}, u32[]{:S(2)}) %collective-permute-start) | collective-permute-done | bytes 262176 | tf_op jit(solution)/shard_map/ppermute | solution.py:281
  34.0 0.2 collective-permute-start.1
  34.2 1.2 %collective-permute-done.1.other_ref = bf16[32,2048]{1,0:T(8,128)(2,1)S(1)} collective-permute-done((bf16[32,2048]{1,0:T(8,128)(2,1)S(1)}, bf16[32,2048]{1,0:T(8,128)(2,1)S(1)}, u32[]{:S(2)}, u32[]{:S(2)}) %collective-permute-start.1) | collective-permute-done | bytes 131104 | tf_op jit(solution)/shard_map/ppermute | solution.py:281
  35.4 1.4 %functions.1 = bf16[4,64,256]{2,1,0:T(8,128)(2,1)S(1)} custom-call(bf16[32,2048]{1,0:T(8,128)(2,1)S(1)} %act.1.mine_ref, bf16[32,2048]{1,0:T(8,128)(2,1)S(1)} %collective-permute-done.1.other_ref, bf16[4,256,2048]{2,1,0:T(8,128)(2,1)S(1)} %copy-done.2), custom_call_target="tpu_custom_call" | custom-call | flops 268435456 | bytes 4194304 | tf_op jit(solution)/shard_map/functions/pallas_call | solution.py:198
  36.8 8.9 %all_to_all.17 = bf16[4,64,256]{2,1,0:T(8,128)(2,1)S(1)} all-to-all(bf16[4,64,256]{2,1,0:T(8,128)(2,1)S(1)} %functions.1), channel_id=1, replica_groups={{0,2,4,6},{1,3,5,7},{8,10,12,14},{9,11,13,15},{16,18,20,22},{17,19,21,2..., dimensions={0} | all-to-all | bytes 262144 | tf_op jit(solution)/shard_map/all_to_all | solution.py:286
  45.7 0.9 %collective-permute-start.2 = (bf16[256,256]{1,0:T(8,128)(2,1)S(1)}, bf16[256,256]{1,0:T(8,128)(2,1)S(1)}, u32[]{:S(2)}, u32[]{:S(2)}) collective-permute-start(bf16[256,256]{1,0:T(8,128)(2,1)S(1)} %bitcast.5), channel_id=1, source_target_pairs={{0,8},{8,0},{16,24},{24,16},{1,9},{9,1},{17,25},{25,17},{2,10},{10... | collective-permute-start | bytes 393224 | tf_op jit(solution)/shard_map/ppermute | solution.py:281
  46.6 0.6 %collective-permute-start.3 = (bf16[256,256]{1,0:T(8,128)(2,1)S(1)}, bf16[256,256]{1,0:T(8,128)(2,1)S(1)}, u32[]{:S(2)}, u32[]{:S(2)}) collective-permute-start(bf16[256,256]{1,0:T(8,128)(2,1)S(1)} %bitcast.6), channel_id=1, source_target_pairs={{0,16},{8,24},{16,0},{24,8},{1,17},{9,25},{17,1},{25,9},{2,18},{10... | collective-permute-start | bytes 393224 | tf_op jit(solution)/shard_map/ppermute | solution.py:281
  47.2 2.0 %collective-permute-start.4 = (bf16[256,256]{1,0:T(8,128)(2,1)S(1)}, bf16[256,256]{1,0:T(8,128)(2,1)}, u32[]{:S(2)}, u32[]{:S(2)}) collective-permute-start(bf16[256,256]{1,0:T(8,128)(2,1)S(1)} %bitcast.7), channel_id=1, source_target_pairs={{0,24},{8,16},{16,8},{24,0},{1,25},{9,17},{17,9},{25,1},{2,26},{10... | collective-permute-start | bytes 393224 | tf_op jit(solution)/shard_map/ppermute | solution.py:281
  49.2 0.2 copy.10.row_ref
  49.4 0.9 %backward_own.1.total_ref = f32[1024,256]{1,0:T(8,128)S(1)} custom-call(s32[16]{0:T(128)S(1)} %copy-done.4, bf16[1024,1024]{1,0:T(8,128)(2,1)S(1)} %get-tuple-element.11.rolled_ref, bf16[256,256]{1,0:T(8,128)(2,1)S(1)} %bitcast.8, bf16[1024,256]{1,0:T(8,128)(2,1)S(1)} %copy-done.3, f32[1024,1]{1,0:T(8,128)S(1)} %copy.10.row_ref, f32[1,256]{1,0:T(1,128)S(1)} %bitcast.9), custom_call_target="tpu_custom_call" | custom-call | flops 134217728 | bytes 4194304 | tf_op jit(solution)/shard_map/backward_own/pallas_call | solution.py:226
  50.3 1.1 %collective-permute-done.2.refs_0_ = bf16[256,256]{1,0:T(8,128)(2,1)S(1)} collective-permute-done((bf16[256,256]{1,0:T(8,128)(2,1)S(1)}, bf16[256,256]{1,0:T(8,128)(2,1)S(1)}, u32[]{:S(2)}, u32[]{:S(2)}) %collective-permute-start.2) | collective-permute-done | bytes 131104 | tf_op jit(solution)/shard_map/ppermute | solution.py:281
  51.4 0.3 collective-permute-done.3.refs_1_
  51.7 1.5 %collective-permute-done.4.refs_2_ = bf16[256,256]{1,0:T(8,128)(2,1)} collective-permute-done((bf16[256,256]{1,0:T(8,128)(2,1)S(1)}, bf16[256,256]{1,0:T(8,128)(2,1)}, u32[]{:S(2)}, u32[]{:S(2)}) %collective-permute-start.4) | collective-permute-done | bytes 131104 | tf_op jit(solution)/shard_map/ppermute | solution.py:281
  53.2 2.4 %backward_rest.1 = f32[1024,256]{1,0:T(8,128)} custom-call(s32[16]{0:T(128)S(1)} %copy-done.4, f32[1024,256]{1,0:T(8,128)S(1)} %backward_own.1.total_ref, bf16[1024,1024]{1,0:T(8,128)(2,1)S(1)} %get-tuple-element.11.rolled_ref, bf16[256,256]{1,0:T(8,128)(2,1)S(1)} %collective-permute-done.2.refs_0_, bf16[256,256]{1,0:T(8,128)(2,1)S(1)} %collective-permute-done.3.refs_1_, ...), custom_call_target="tpu_custom_call" | custom-call | flops 536870912 | bytes 4194304 | tf_op jit(solution)/shard_map/backward_rest/pallas_call | solution.py:268
  (11 shorter events, 0.1 us)
Async XLA Ops:
  3.1 2.0 %copy-start = (bf16[4,256,2048]{2,1,0:T(8,128)(2,1)}, bf16[4,256,2048]{2,1,0:T(8,128)(2,1)S(1)}, u32[]{:S(2)}) copy-start(bf16[4,256,2048]{2,1,0:T(8,128)(2,1)S(1)} %get-tuple-element.13.basis_ref) | copy-start | bytes 12582916
  29.2 2.2 %copy-start.1 = (bf16[4,256,2048]{2,1,0:T(8,128)(2,1)S(1)}, bf16[4,256,2048]{2,1,0:T(8,128)(2,1)}, u32[]{:S(2)}) copy-start(bf16[4,256,2048]{2,1,0:T(8,128)(2,1)} %copy-done) | copy-start | bytes 12582916
  31.4 4.0 %copy-start.2 = (bf16[4,256,2048]{2,1,0:T(8,128)(2,1)S(1)}, bf16[4,256,2048]{2,1,0:T(8,128)(2,1)}, u32[]{:S(2)}) copy-start(bf16[4,256,2048]{2,1,0:T(8,128)(2,1)} %copy-done) | copy-start | bytes 12582916
  31.4 17.7 %copy-start.6 = (f32[1024]{0:T(1024)S(1)}, f32[1024]{0:T(1024)}, u32[]{:S(2)}) copy-start(f32[1024]{0:T(1024)} %param.10) | copy-start | bytes 12292
  32.3 17.1 %copy-start.3 = (bf16[1024,256]{1,0:T(8,128)(2,1)S(1)}, bf16[1024,256]{1,0:T(8,128)(2,1)}, u32[]{:S(2)}) copy-start(bf16[1024,256]{1,0:T(8,128)(2,1)} %coeff_ref.1) | copy-start | bytes 1572868
  32.3 17.1 %copy-start.4 = (s32[16]{0:T(128)S(1)}, s32[16]{0:T(128)}, u32[]{:S(2)}) copy-start(s32[16]{0:T(128)} %pad_ref.3) | copy-start | bytes 196
  32.3 17.1 %copy-start.5 = (f32[256]{0:T(256)S(1)}, f32[256]{0:T(256)}, u32[]{:S(2)}) copy-start(f32[256]{0:T(256)} %param.11) | copy-start | bytes 3076
  32.3 1.6 %collective-permute-start = (f32[32,2048]{1,0:T(8,128)S(1)}, f32[32,2048]{1,0:T(8,128)S(1)}, u32[]{:S(2)}, u32[]{:S(2)}) collective-permute-start(f32[32,2048]{1,0:T(8,128)S(1)} %get-tuple-element.15), channel_id=1, source_target_pairs={{0,1},{1,0},{2,3},{3,2},{4,5},{5,4},{6,7},{7,6},{8,9},{9,8},{10,11... | collective-permute-start | bytes 786440 | tf_op jit(solution)/shard_map/ppermute | solution.py:281
  34.0 1.4 %collective-permute-start.1 = (bf16[32,2048]{1,0:T(8,128)(2,1)S(1)}, bf16[32,2048]{1,0:T(8,128)(2,1)S(1)}, u32[]{:S(2)}, u32[]{:S(2)}) collective-permute-start(bf16[32,2048]{1,0:T(8,128)(2,1)S(1)} %act.1.mine_ref), channel_id=1, source_target_pairs={{0,1},{1,0},{2,3},{3,2},{4,5},{5,4},{6,7},{7,6},{8,9},{9,8},{10,11... | collective-permute-start | bytes 393224 | tf_op jit(solution)/shard_map/ppermute | solution.py:281
  45.7 5.7 %collective-permute-start.2 = (bf16[256,256]{1,0:T(8,128)(2,1)S(1)}, bf16[256,256]{1,0:T(8,128)(2,1)S(1)}, u32[]{:S(2)}, u32[]{:S(2)}) collective-permute-start(bf16[256,256]{1,0:T(8,128)(2,1)S(1)} %bitcast.5), channel_id=1, source_target_pairs={{0,8},{8,0},{16,24},{24,16},{1,9},{9,1},{17,25},{25,17},{2,10},{10... | collective-permute-start | bytes 393224 | tf_op jit(solution)/shard_map/ppermute | solution.py:281
  46.6 5.1 %collective-permute-start.3 = (bf16[256,256]{1,0:T(8,128)(2,1)S(1)}, bf16[256,256]{1,0:T(8,128)(2,1)S(1)}, u32[]{:S(2)}, u32[]{:S(2)}) collective-permute-start(bf16[256,256]{1,0:T(8,128)(2,1)S(1)} %bitcast.6), channel_id=1, source_target_pairs={{0,16},{8,24},{16,0},{24,8},{1,17},{9,25},{17,1},{25,9},{2,18},{10... | collective-permute-start | bytes 393224 | tf_op jit(solution)/shard_map/ppermute | solution.py:281
  47.2 6.0 %collective-permute-start.4 = (bf16[256,256]{1,0:T(8,128)(2,1)S(1)}, bf16[256,256]{1,0:T(8,128)(2,1)}, u32[]{:S(2)}, u32[]{:S(2)}) collective-permute-start(bf16[256,256]{1,0:T(8,128)(2,1)S(1)} %bitcast.7), channel_id=1, source_target_pairs={{0,24},{8,16},{16,8},{24,0},{1,25},{9,17},{17,9},{25,1},{2,26},{10... | collective-permute-start | bytes 393224 | tf_op jit(solution)/shard_map/ppermute | solution.py:281

commit v3 on v1

v3 whole, which is shorter than its diff:
```python
import functools

import jax
import jax.numpy as jnp
from jax import lax
from jax.experimental import pallas as pl
from jax.experimental.pallas import tpu as pltpu
from jax.sharding import PartitionSpec as P

MIB = 1024 * 1024
HBM = pl.BlockSpec(memory_space=pltpu.HBM)
VMEM = pl.BlockSpec(memory_space=pltpu.VMEM)
BF16 = jnp.bfloat16
F32 = jnp.float32
LONG = 8


def call(kernel, name, out_shape, in_specs, out_specs, scratch=(), flops=0, moved=0, mib=16):
    return pl.pallas_call(
        kernel,
        out_shape=out_shape,
        in_specs=in_specs,
        out_specs=out_specs,
        scratch_shapes=scratch,
        compiler_params=pltpu.CompilerParams(vmem_limit_bytes=mib * MIB),
        cost_estimate=pl.CostEstimate(flops=flops, bytes_accessed=moved, transcendentals=0),
        name=name,
    )


def in_hbm(value):
    return pltpu.with_memory_space_constraint(value, pltpu.HBM)


def array(shape, dtype):
    return jax.ShapeDtypeStruct(shape, dtype)


def dot(left, right):
    return jnp.dot(left, right, preferred_element_type=F32)


def dot_turned(left, right):
    return lax.dot_general(left, right, (((1,), (1,)), ((), ())), preferred_element_type=F32)


def chunk_of(turned_ref, rolled_ref, wide, k):
    own = rolled_ref.shape[1] // wide
    start = pl.multiple_of((lax.axis_index("wide") ^ k) * own, own)
    return dot(turned_ref[...], rolled_ref[:, pl.ds(start, own)])


def first_kernel(
    wide,
    level_hbm,
    pad_hbm,
    shift_hbm,
    coeff_hbm,
    table_hbm,
    out_ref,
    turned_ref,
    rolled_ref,
    level_ref,
    pad_ref,
    shift_ref,
    coeff_ref,
    table_ref,
    sems,
):
    pairs = [
        (level_hbm, level_ref),
        (shift_hbm, shift_ref),
        (pad_hbm, pad_ref),
        (table_hbm, table_ref),
        (coeff_hbm, coeff_ref),
    ]
    copies = [
        pltpu.make_async_copy(source, target, sems.at[i])
        for i, (source, target) in enumerate(pairs)
    ]
    for copy in copies:
        copy.start()
    for copy in copies[:4]:
        copy.wait()
    slots = pad_ref.shape[0]
    width = table_ref.shape[1]
    for s in range(slots):
        rows = slice(s * width, (s + 1) * width)
        rolled_ref[rows, :] = pltpu.roll(table_ref[level_ref[s]], shift_ref[s], 1)
    copies[4].wait()
    row = lax.broadcasted_iota(jnp.int32, (width, coeff_ref.shape[1]), 0)
    pieces = []
    for s in range(slots):
        rows = slice(s * width, (s + 1) * width)
        piece = coeff_ref[rows, :].astype(F32)
        pieces.append(jnp.where(row < width - pad_ref[s], piece, 0.0).astype(BF16))
    turned_ref[...] = jnp.concatenate(pieces, axis=0).T
    out_ref[...] = chunk_of(turned_ref, rolled_ref, wide, wide - 1).astype(BF16).T


def first(wide, level, pad, shift, coeff, tables):
    rows, columns = coeff.shape
    points = tables.shape[2]
    slots = pad.shape[0]
    inputs = (level, pad, shift, coeff, tables)
    return call(
        functools.partial(first_kernel, wide),
        "forward_first",
        (
            array((points // wide, columns), BF16),
            array((columns, rows), BF16),
            array((rows, points), BF16),
        ),
        [HBM] * 5,
        (VMEM,) * 3,
        [
            pltpu.SMEM((slots,), jnp.int32),
            pltpu.SMEM((slots,), jnp.int32),
            pltpu.SMEM((slots,), jnp.int32),
            pltpu.VMEM(coeff.shape, coeff.dtype),
            pltpu.VMEM(tables.shape, tables.dtype),
            pltpu.SemaphoreType.DMA((5,)),
        ],
        flops=2 * rows * points // wide * columns,
        moved=4 * MIB,
    )(*(in_hbm(value) for value in inputs))


def chunk_kernel(wide, k, turned_ref, rolled_ref, out_ref):
    out_ref[...] = chunk_of(turned_ref, rolled_ref, wide, k).astype(BF16).T


def chunk(wide, k, turned, rolled):
    columns, rows = turned.shape
    own = rolled.shape[1] // wide
    return call(
        functools.partial(chunk_kernel, wide, k),
        "forward_chunk",
        array((own, columns), BF16),
        [VMEM] * 2,
        VMEM,
        flops=2 * rows * own * columns * LONG,
        moved=MIB * LONG,
    )(turned, rolled)


def last_kernel(
    wide,
    chips,
    turned_ref,
    rolled_ref,
    basis_hbm,
    potential_hbm,
    out_ref,
    basis_ref,
    potential_ref,
    sems,
):
    place = lax.axis_index("narrow")
    core, chip = place % 2, place // 2
    columns = turned_ref.shape[0]
    pairs = []
    for j in range(chips):
        start = pl.multiple_of(((chip ^ j) * 2 + core) * columns, columns)
        pairs.append((basis_hbm.at[pl.ds(start, columns), :], basis_ref.at[j]))
    pairs.append((potential_hbm, potential_ref))
    copies = [
        pltpu.make_async_copy(source, target, sems.at[i])
        for i, (source, target) in enumerate(pairs)
    ]
    for copy in copies:
        copy.start()
    out_ref[...] = chunk_of(turned_ref, rolled_ref, wide, 0).T
    for copy in copies:
        copy.wait()


def last(wide, chips, turned, rolled, basis, potential):
    columns, rows = turned.shape
    own = rolled.shape[1] // wide
    return call(
        functools.partial(last_kernel, wide, chips),
        "forward_own",
        (
            array((own, columns), F32),
            array((chips, columns, basis.shape[1]), BF16),
            array(potential.shape, F32),
        ),
        [VMEM, VMEM, HBM, HBM],
        (VMEM,) * 3,
        [pltpu.SemaphoreType.DMA((chips + 1,))],
        flops=2 * rows * own * columns,
        moved=10 * MIB,
    )(turned, rolled, in_hbm(basis), in_hbm(potential))


def combine_kernel(wide, chips, *refs):
    parts, outs = refs[:wide], refs[wide:]
    chip = lax.axis_index("narrow") // 2
    rows = outs[0].shape[0]
    for j in range(chips):
        start = pl.multiple_of((chip ^ j) * rows, rows)
        total = parts[0][pl.ds(start, rows), :]
        for part in parts[1:]:
            total = total + part[pl.ds(start, rows), :].astype(F32)
        outs[j][...] = total.astype(BF16)


def combine(chips, parts):
    rows, columns = parts[0].shape
    wide = len(parts)
    return call(
        functools.partial(combine_kernel, wide, chips),
        "wide_sum",
        tuple(array((rows // chips, columns), BF16) for _ in range(chips)),
        [VMEM] * wide,
        (VMEM,) * chips,
        moved=MIB,
    )(*parts)


def own_points_kernel(x_ref, basis_ref, out_ref):
    out_ref[...] = dot(x_ref[...], basis_ref[0])


def own_points(x, basis):
    rows = x.shape[0]
    points = basis.shape[2]
    return call(
        own_points_kernel,
        "points_own",
        array((rows, points), F32),
        [VMEM] * 2,
        VMEM,
        flops=2 * rows * points * x.shape[1],
        moved=2 * MIB,
    )(x, basis)


def more_points_kernel(j, total_ref, x_ref, basis_ref, out_ref):
    out_ref[...] = total_ref[...] + dot(x_ref[...], basis_ref[j])


def more_points(j, total, x, basis):
    rows, points = total.shape
    return call(
        functools.partial(more_points_kernel, j),
        "points_more",
        array((rows, points), F32),
        [VMEM] * 3,
        VMEM,
        flops=2 * rows * points * x.shape[1],
        moved=2 * MIB,
    )(total, x, basis)


def last_points_kernel(j, total_ref, x_ref, basis_ref, mine_ref, theirs_ref):
    core = lax.axis_index("narrow") % 2
    rows = mine_ref.shape[0]
    total = total_ref[...] + dot(x_ref[...], basis_ref[j])
    low, high = total[:rows], total[rows:]
    mine_ref[...] = jnp.where(core == 0, low, high)
    theirs_ref[...] = jnp.where(core == 0, high, low)


def last_points(j, total, x, basis):
    rows, points = total.shape
    half = array((rows // 2, points), F32)
    return call(
        functools.partial(last_points_kernel, j),
        "points_last",
        (half, half),
        [VMEM] * 3,
        (VMEM, VMEM),
        flops=2 * rows * points * x.shape[1],
        moved=2 * MIB,
    )(total, x, basis)


def act_kernel(mine_ref, other_ref, potential_ref, out_ref):
    on_grid = mine_ref[...] + other_ref[...]
    out_ref[...] = (potential_ref[...] * on_grid).astype(BF16)


def act(mine, other, potential):
    return call(
        act_kernel, "act", array(mine.shape, BF16), [VMEM] * 3, VMEM, moved=MIB
    )(mine, other, potential)


def first_functions_kernel(j, mine_ref, other_ref, basis_ref, out_ref, both_ref):
    core = lax.axis_index("narrow") % 2
    rows = mine_ref.shape[0]
    mine, other = mine_ref[...].astype(F32), other_ref[...].astype(F32)
    both_ref[:rows] = jnp.where(core == 0, mine, other).astype(BF16)
    both_ref[rows:] = jnp.where(core == 0, other, mine).astype(BF16)
    out_ref[...] = dot_turned(both_ref[...], basis_ref[j]).astype(BF16)


def first_functions(j, mine, other, basis):
    rows, points = mine.shape
    columns = basis.shape[1]
    return call(
        functools.partial(first_functions_kernel, j),
        "functions_first",
        (array((2 * rows, columns), BF16), array((2 * rows, points), BF16)),
        [VMEM] * 3,
        (VMEM, VMEM),
        flops=4 * rows * points * columns,
        moved=2 * MIB,
    )(mine, other, basis)


def functions_kernel(j, both_ref, basis_ref, out_ref):
    out_ref[...] = dot_turned(both_ref[...], basis_ref[j]).astype(BF16)


def functions(j, both, basis):
    rows, points = both.shape
    columns = basis.shape[1]
    long = LONG if j else 1
    return call(
        functools.partial(functions_kernel, j),
        "functions_more",
        array((rows, columns), BF16),
        [VMEM] * 2,
        VMEM,
        flops=2 * rows * points * columns * long,
        moved=2 * MIB * long,
    )(both, basis)


def assemble_kernel(*refs):
    parts, out_ref = refs[:-1], refs[-1]
    chip = lax.axis_index("narrow") // 2
    rows = parts[0].shape[0]
    for j, part in enumerate(parts):
        start = pl.multiple_of((chip ^ j) * rows, rows)
        out_ref[pl.ds(start, rows), :] = part[...]


def assemble(parts):
    rows, columns = parts[0].shape
    chips = len(parts)
    return call(
        assemble_kernel,
        "assemble",
        array((rows * chips, columns), BF16),
        [VMEM] * chips,
        VMEM,
        moved=MIB // 4,
    )(*parts)


def own_kernel(wide, pad_ref, rolled_ref, grid_ref, coeff_ref, row_ref, column_ref, out_ref):
    slots = pad_ref.shape[0]
    width = rolled_ref.shape[0] // slots
    me = lax.axis_index("wide")
    own = rolled_ref.shape[1] // wide
    start = pl.multiple_of(me * own, own)
    out_ref[...] = dot(rolled_ref[:, pl.ds(start, own)], grid_ref[...])
    for s in range(slots):
        rows = slice(s * width, (s + 1) * width)
        energy = row_ref[rows, :] + column_ref[...]
        out_ref[rows, :] += energy * coeff_ref[rows, :].astype(F32)


def backward_own(wide, pad, rolled, grid, coeff, row_energy, column_energy):
    smem = pl.BlockSpec(memory_space=pltpu.SMEM)
    rows, columns = coeff.shape
    return call(
        functools.partial(own_kernel, wide),
        "backward_own",
        array(coeff.shape, F32),
        [smem] + [VMEM] * 5,
        VMEM,
        flops=2 * rows * columns * rolled.shape[1] // wide,
        moved=4 * MIB,
    )(pad, rolled, grid, coeff, row_energy[:, None], column_energy[None, :])


def more_kernel(wide, k, total_ref, rolled_ref, grid_ref, out_ref):
    own = rolled_ref.shape[1] // wide
    start = pl.multiple_of((lax.axis_index("wide") ^ k) * own, own)
    out_ref[...] = total_ref[...] + dot(rolled_ref[:, pl.ds(start, own)], grid_ref[...])


def backward_more(wide, k, total, rolled, grid):
    rows, columns = total.shape
    return call(
        functools.partial(more_kernel, wide, k),
        "backward_more",
        array(total.shape, F32),
        [VMEM] * 3,
        VMEM,
        flops=2 * rows * columns * rolled.shape[1] // wide,
        moved=3 * MIB,
    )(total, rolled, grid)


def end_kernel(wide, k, pad_ref, total_ref, rolled_ref, grid_ref, out_hbm, out_ref, sems):
    slots = pad_ref.shape[0]
    width = rolled_ref.shape[0] // slots
    own = rolled_ref.shape[1] // wide
    start = pl.multiple_of((lax.axis_index("wide") ^ k) * own, own)
    steps = sems.shape[0]
    rows = rolled_ref.shape[0] // steps
    row = lax.broadcasted_iota(jnp.int32, (width, out_ref.shape[1]), 0)
    copies = []
    for i in range(steps):
        span = pl.ds(i * rows, rows)
        total = total_ref[span, :] + dot(rolled_ref[span, pl.ds(start, own)], grid_ref[...])
        for s in range(rows // width):
            slot = i * (rows // width) + s
            value = total[s * width : (s + 1) * width, :]
            out_ref[pl.ds(slot * width, width), :] = jnp.where(
                row < width - pad_ref[slot], value, 0.0
            )
        copies.append(pltpu.make_async_copy(out_ref.at[span, :], out_hbm.at[span, :], sems.at[i]))
        copies[-1].start()
    for copy in copies:
        copy.wait()


def backward_end(wide, k, pad, total, rolled, grid):
    smem = pl.BlockSpec(memory_space=pltpu.SMEM)
    rows, columns = total.shape
    return call(
        functools.partial(end_kernel, wide, k),
        "backward_end",
        array(total.shape, F32),
        [smem] + [VMEM] * 3,
        HBM,
        [pltpu.VMEM(total.shape, F32), pltpu.SemaphoreType.DMA((4,))],
        flops=2 * rows * columns * rolled.shape[1] // wide,
        moved=4 * MIB,
    )(pad, total, rolled, grid)


def exchange(value, step, size, axis):
    return lax.ppermute(value, axis, [(i, i ^ step) for i in range(size)])


def body(
    wide,
    narrow,
    coeff,
    groupb_row_energy,
    groupa_energy,
    groupb_basis_values,
    basis_a,
    potential,
    slot_sparse_level,
    block_pad,
    slot_grid_offset,
):
    chips = narrow // 2
    tables = jnp.swapaxes(groupb_basis_values, 1, 2)
    far, turned, rolled = first(
        wide, slot_sparse_level, block_pad, slot_grid_offset, coeff, tables
    )
    arrived = {wide - 1: exchange(far, wide - 1, wide, "wide")}
    for k in range(1, wide - 1):
        arrived[k] = exchange(chunk(wide, k, turned, rolled), k, wide, "wide")
    mine, basis, pot = last(wide, chips, turned, rolled, basis_a, potential)
    pieces = combine(chips, [mine] + [arrived[k] for k in range(1, wide)])
    xs = [exchange(pieces[j], 2 * j, narrow, "narrow") for j in range(1, chips)]
    total = own_points(pieces[0], basis)
    for j in range(1, chips - 1):
        total = more_points(j, total, xs[j - 1], basis)
    mine, theirs = last_points(chips - 1, total, xs[-1], basis)
    acted = act(mine, exchange(theirs, 1, narrow, "narrow"), pot)
    other = exchange(acted, 1, narrow, "narrow")
    block, both = first_functions(chips - 1, acted, other, basis)
    sent = {chips - 1: exchange(block, 2 * (chips - 1), narrow, "narrow")}
    for j in reversed(range(1, chips - 1)):
        sent[j] = exchange(functions(j, both, basis), 2 * j, narrow, "narrow")
    grid = assemble([functions(0, both, basis)] + [sent[j] for j in range(1, chips)])
    grids = [exchange(grid, k, wide, "wide") for k in range(1, wide)]
    total = backward_own(
        wide, block_pad, rolled, grid, coeff, groupb_row_energy, groupa_energy
    )
    for k in range(1, wide - 1):
        total = backward_more(wide, k, total, rolled, grids[k - 1])
    return backward_end(wide, wide - 1, block_pad, total, rolled, grids[-1])


def solution(mesh):
    return jax.shard_map(
        functools.partial(body, mesh.shape["wide"], mesh.shape["narrow"]),
        mesh=mesh,
        in_specs=(
            P("wide", "narrow"),
            P("wide"),
            P("narrow"),
            P(),
            P(),
            P(("wide", "narrow"), None),
            P("wide"),
            P("wide"),
            P("wide"),
        ),
        out_specs=P("wide", "narrow"),
        check_vma=False,
    )
```

time: 46.3 us -> 45.3 us (0.978)
  waiting for transfers between devices: 19.2 us -> 14.8 us
  Pallas kernels: 9.3 us -> 12.5 us
    ppermute x14, waiting for transfers between devices: 19.2 us -> 14.8 us  [exchange(): return lax.ppermute(value, axis, [(i, i ^ step) for i in range(size)])]
    pallas_call x7 -> x15, Pallas kernels: 8.34 us -> 11.6 us  [the longest x1 2.39 us: last(): call(functools.partial(last_kernel, wide, chips), 'forward_own', (array((...]
  transfers between devices with their start and end apart: 14 -> 14, of which waited for: 11 -> 8; matrix products, arithmetic and copies ran while one was open for 0% -> 0% of each run, Pallas kernels for 3% -> 14%
where the time goes in v3:
time: 45.3 us; the launch traced here: 45.2 us
  starting transfers between devices  17.4 us (38%)
  waiting for transfers between devices  14.8 us (33%)
  Pallas kernels  12.5 us (28%)
    ppermute x14, starting transfers between devices, exchange(): return lax.ppermute(value, axis, [(i, i ^ step) for i in range(size)])  17.4 us
    ppermute x14, waiting for transfers between devices, exchange(): return lax.ppermute(value, axis, [(i, i ^ step) for i in range(size)])  14.8 us
    pallas_call x1, Pallas kernels, last(): call(functools.partial(last_kernel, wide, chips), 'forward_own', (array((...  2.39 us
    pallas_call x1, Pallas kernels, first(): call(functools.partial(first_kernel, wide), 'forward_first', (array((poin...  2.21 us
    pallas_call x1, Pallas kernels, backward_end(): call(functools.partial(end_kernel, wide, k), 'backward_end', array(total....  1.78 us
    pallas_call x2, Pallas kernels, backward_more(): call(functools.partial(more_kernel, wide, k), 'backward_more', array(tota...  1.49 us
    pallas_call x3, Pallas kernels, functions(): call(functools.partial(functions_kernel, j), 'functions_more', array((row...  1.33 us
  transfers between devices with their start and end apart: 14, of which 8 were waited for; matrix products, arithmetic and copies ran while one was open for 0% of the time, Pallas kernels for 14%

profile of v3, /device:TPU:0, one launch (start us, length us, event | category | flops | bytes accessed | tf_op | source)
XLA Modules:
  0.0 45.2 jit_solution(13218397168281576208)
XLA Ops:
  0.0 2.2 %forward_first.1 = (bf16[256,256]{1,0:T(8,128)(2,1)S(1)}, bf16[256,1024]{1,0:T(8,128)(2,1)S(1)}, bf16[1024,1024]{1,0:T(8,128)(2,1)S(1)}) custom-call(s32[16]{0:T(128)} %level_hbm.1, s32[16]{0:T(128)} %pad_ref.3, s32[16]{0:T(128)} %shift_hbm.1, bf16[1024,256]{1,0:T(8,128)(2,1)} %coeff_ref.1, bf16[4,64,1024]{2,1,0:T(8,128)(2,1)} %bitcast.4), custom_call_target="tpu_custom_call" | custom-call | flops 134217728 | bytes 4194304 | tf_op jit(solution)/shard_map/forward_first/pallas_call | solution.py:106
  2.6 3.0 %collective-permute-start = (bf16[256,256]{1,0:T(8,128)(2,1)S(1)}, bf16[256,256]{1,0:T(8,128)(2,1)S(1)}, u32[]{:S(2)}, u32[]{:S(2)}) collective-permute-start(bf16[256,256]{1,0:T(8,128)(2,1)S(1)} %forward_chunk.2), channel_id=1, source_target_pairs={{0,8},{8,0},{16,24},{24,16},{1,9},{9,1},{17,25},{25,17},{2,10},{10... | collective-permute-start | bytes 393224 | tf_op jit(solution)/shard_map/ppermute | solution.py:441
  6.0 1.6 %collective-permute-start.1 = (bf16[256,256]{1,0:T(8,128)(2,1)S(1)}, bf16[256,256]{1,0:T(8,128)(2,1)S(1)}, u32[]{:S(2)}, u32[]{:S(2)}) collective-permute-start(bf16[256,256]{1,0:T(8,128)(2,1)S(1)} %forward_chunk.3), channel_id=1, source_target_pairs={{0,16},{8,24},{16,0},{24,8},{1,17},{9,25},{17,1},{25,9},{2,18},{10... | collective-permute-start | bytes 393224 | tf_op jit(solution)/shard_map/ppermute | solution.py:441
  7.6 2.4 %forward_own.1 = (f32[256,256]{1,0:T(8,128)S(1)}, bf16[4,256,2048]{2,1,0:T(8,128)(2,1)S(1)}, f32[32,2048]{1,0:T(8,128)S(1)}) custom-call(bf16[256,1024]{1,0:T(8,128)(2,1)S(1)} %get-tuple-element.20.turned_ref, bf16[1024,1024]{1,0:T(8,128)(2,1)S(1)} %get-tuple-element.19.rolled_ref, bf16[2048,2048]{1,0:T(8,128)(2,1)} %basis_hbm.1, f32[32,2048]{1,0:T(8,128)} %potential_hbm.1), custom_call_target="tpu_custom_call" | custom-call | flops 134217728 | bytes 10485760 | tf_op jit(solution)/shard_map/forward_own/pallas_call | solution.py:181
  10.0 3.8 %collective-permute-done.1.refs_2_ = bf16[256,256]{1,0:T(8,128)(2,1)S(1)} collective-permute-done((bf16[256,256]{1,0:T(8,128)(2,1)S(1)}, bf16[256,256]{1,0:T(8,128)(2,1)S(1)}, u32[]{:S(2)}, u32[]{:S(2)}) %collective-permute-start.1) | collective-permute-done | bytes 131104 | tf_op jit(solution)/shard_map/ppermute | solution.py:441
  13.9 1.6 %collective-permute-start.3 = (bf16[64,256]{1,0:T(8,128)(2,1)S(1)}, bf16[64,256]{1,0:T(8,128)(2,1)S(1)}, u32[]{:S(2)}, u32[]{:S(2)}) collective-permute-start(bf16[64,256]{1,0:T(8,128)(2,1)S(1)} %get-tuple-element.25), channel_id=1, source_target_pairs={{0,2},{1,3},{2,0},{3,1},{4,6},{5,7},{6,4},{7,5},{8,10},{9,11},{10,... | collective-permute-start | bytes 98312 | tf_op jit(solution)/shard_map/ppermute | solution.py:441
  15.5 2.6 %collective-permute-start.4 = (bf16[64,256]{1,0:T(8,128)(2,1)S(1)}, bf16[64,256]{1,0:T(8,128)(2,1)S(1)}, u32[]{:S(2)}, u32[]{:S(2)}) collective-permute-start(bf16[64,256]{1,0:T(8,128)(2,1)S(1)} %get-tuple-element.26), channel_id=1, source_target_pairs={{0,4},{1,5},{2,6},{3,7},{4,0},{5,1},{6,2},{7,3},{8,12},{9,13},{10,... | collective-permute-start | bytes 98312 | tf_op jit(solution)/shard_map/ppermute | solution.py:441
  19.0 2.0 %collective-permute-done.4.x_ref = bf16[64,256]{1,0:T(8,128)(2,1)S(1)} collective-permute-done((bf16[64,256]{1,0:T(8,128)(2,1)S(1)}, bf16[64,256]{1,0:T(8,128)(2,1)S(1)}, u32[]{:S(2)}, u32[]{:S(2)}) %collective-permute-start.4) | collective-permute-done | bytes 32800 | tf_op jit(solution)/shard_map/ppermute | solution.py:441
  21.2 2.6 %collective-permute-done.5.x_ref = bf16[64,256]{1,0:T(8,128)(2,1)S(1)} collective-permute-done((bf16[64,256]{1,0:T(8,128)(2,1)S(1)}, bf16[64,256]{1,0:T(8,128)(2,1)S(1)}, u32[]{:S(2)}, u32[]{:S(2)}) %collective-permute-start.5) | collective-permute-done | bytes 32800 | tf_op jit(solution)/shard_map/ppermute | solution.py:441
  24.2 1.5 %collective-permute-done.6.other_ref = f32[32,2048]{1,0:T(8,128)S(1)} collective-permute-done((f32[32,2048]{1,0:T(8,128)S(1)}, f32[32,2048]{1,0:T(8,128)S(1)}, u32[]{:S(2)}, u32[]{:S(2)}) %collective-permute-start.6) | collective-permute-done | bytes 262176 | tf_op jit(solution)/shard_map/ppermute | solution.py:441
  26.0 1.2 %collective-permute-done.7.other_ref = bf16[32,2048]{1,0:T(8,128)(2,1)S(1)} collective-permute-done((bf16[32,2048]{1,0:T(8,128)(2,1)S(1)}, bf16[32,2048]{1,0:T(8,128)(2,1)S(1)}, u32[]{:S(2)}, u32[]{:S(2)}) %collective-permute-start.7) | collective-permute-done | bytes 131104 | tf_op jit(solution)/shard_map/ppermute | solution.py:441
  27.2 0.4 functions_first.1
  27.7 0.4 functions_more.5
  28.7 0.9 %collective-permute-start.8 = (bf16[64,256]{1,0:T(8,128)(2,1)S(1)}, bf16[64,256]{1,0:T(8,128)(2,1)S(1)}, u32[]{:S(2)}, u32[]{:S(2)}) collective-permute-start(bf16[64,256]{1,0:T(8,128)(2,1)S(1)} %functions_more.4), channel_id=1, source_target_pairs={{0,2},{1,3},{2,0},{3,1},{4,6},{5,7},{6,4},{7,5},{8,10},{9,11},{10,... | collective-permute-start | bytes 98312 | tf_op jit(solution)/shard_map/ppermute | solution.py:441
  29.6 3.5 %collective-permute-start.10 = (bf16[64,256]{1,0:T(8,128)(2,1)S(1)}, bf16[64,256]{1,0:T(8,128)(2,1)S(1)}, u32[]{:S(2)}, u32[]{:S(2)}) collective-permute-start(bf16[64,256]{1,0:T(8,128)(2,1)S(1)} %get-tuple-element.32), channel_id=1, source_target_pairs={{0,6},{1,7},{2,4},{3,5},{4,2},{5,3},{6,0},{7,1},{8,14},{9,15},{10,... | collective-permute-start | bytes 98312 | tf_op jit(solution)/shard_map/ppermute | solution.py:441
  33.5 1.8 %collective-permute-done.10.refs_3_ = bf16[64,256]{1,0:T(8,128)(2,1)S(1)} collective-permute-done((bf16[64,256]{1,0:T(8,128)(2,1)S(1)}, bf16[64,256]{1,0:T(8,128)(2,1)S(1)}, u32[]{:S(2)}, u32[]{:S(2)}) %collective-permute-start.10) | collective-permute-done | bytes 32800 | tf_op jit(solution)/shard_map/ppermute | solution.py:441
  35.3 0.8 %collective-permute-start.11 = (bf16[256,256]{1,0:T(8,128)(2,1)S(1)}, bf16[256,256]{1,0:T(8,128)(2,1)}, u32[]{:S(2)}, u32[]{:S(2)}) collective-permute-start(bf16[256,256]{1,0:T(8,128)(2,1)S(1)} %assemble.1.grid_ref), channel_id=1, source_target_pairs={{0,8},{8,0},{16,24},{24,16},{1,9},{9,1},{17,25},{25,17},{2,10},{10... | collective-permute-start | bytes 393224 | tf_op jit(solution)/shard_map/ppermute | solution.py:441
  36.1 1.3 %collective-permute-start.12 = (bf16[256,256]{1,0:T(8,128)(2,1)S(1)}, bf16[256,256]{1,0:T(8,128)(2,1)S(1)}, u32[]{:S(2)}, u32[]{:S(2)}) collective-permute-start(bf16[256,256]{1,0:T(8,128)(2,1)S(1)} %assemble.1.grid_ref), channel_id=1, source_target_pairs={{0,16},{8,24},{16,0},{24,8},{1,17},{9,25},{17,1},{25,9},{2,18},{10... | collective-permute-start | bytes 393224 | tf_op jit(solution)/shard_map/ppermute | solution.py:441
  37.4 1.4 %collective-permute-start.13 = (bf16[256,256]{1,0:T(8,128)(2,1)S(1)}, bf16[256,256]{1,0:T(8,128)(2,1)S(1)}, u32[]{:S(2)}, u32[]{:S(2)}) collective-permute-start(bf16[256,256]{1,0:T(8,128)(2,1)S(1)} %assemble.1.grid_ref), channel_id=1, source_target_pairs={{0,24},{8,16},{16,8},{24,0},{1,25},{9,17},{17,9},{25,1},{2,26},{10... | collective-permute-start | bytes 393224 | tf_op jit(solution)/shard_map/ppermute | solution.py:441
  39.1 0.9 %backward_own.1.total_ref = f32[1024,256]{1,0:T(8,128)S(1)} custom-call(s32[16]{0:T(128)S(1)} %copy-done.1, bf16[1024,1024]{1,0:T(8,128)(2,1)S(1)} %get-tuple-element.19.rolled_ref, bf16[256,256]{1,0:T(8,128)(2,1)S(1)} %assemble.1.grid_ref, bf16[1024,256]{1,0:T(8,128)(2,1)S(1)} %copy-done, f32[1024,1]{1,0:T(8,128)S(1)} %copy.10.row_ref, f32[1,256]{1,0:T(1,128)S(1)} %bitcast.3), custom_call_target="tpu_custom_call" | custom-call | flops 134217728 | bytes 4194304 | tf_op jit(solution)/shard_map/backward_own/pallas_call | solution.py:371
  40.0 1.4 %collective-permute-done.11.grid_ref = bf16[256,256]{1,0:T(8,128)(2,1)} collective-permute-done((bf16[256,256]{1,0:T(8,128)(2,1)S(1)}, bf16[256,256]{1,0:T(8,128)(2,1)}, u32[]{:S(2)}, u32[]{:S(2)}) %collective-permute-start.11) | collective-permute-done | bytes 131104 | tf_op jit(solution)/shard_map/ppermute | solution.py:441
  41.4 1.2 %backward_more.2.total_ref = f32[1024,256]{1,0:T(8,128)S(1)} custom-call(f32[1024,256]{1,0:T(8,128)S(1)} %backward_own.1.total_ref, bf16[1024,1024]{1,0:T(8,128)(2,1)S(1)} %get-tuple-element.19.rolled_ref, bf16[256,256]{1,0:T(8,128)(2,1)} %collective-permute-done.11.grid_ref), custom_call_target="tpu_custom_call" | custom-call | flops 134217728 | bytes 3145728 | tf_op jit(solution)/shard_map/backward_more/pallas_call | solution.py:390
  42.9 0.5 %collective-permute-done.13.grid_ref = bf16[256,256]{1,0:T(8,128)(2,1)S(1)} collective-permute-done((bf16[256,256]{1,0:T(8,128)(2,1)S(1)}, bf16[256,256]{1,0:T(8,128)(2,1)S(1)}, u32[]{:S(2)}, u32[]{:S(2)}) %collective-permute-start.13) | collective-permute-done | bytes 131104 | tf_op jit(solution)/shard_map/ppermute | solution.py:441
  43.4 1.8 %backward_end.1 = f32[1024,256]{1,0:T(8,128)} custom-call(s32[16]{0:T(128)S(1)} %copy-done.1, f32[1024,256]{1,0:T(8,128)S(1)} %backward_more.3.total_ref, bf16[1024,1024]{1,0:T(8,128)(2,1)S(1)} %get-tuple-element.19.rolled_ref, bf16[256,256]{1,0:T(8,128)(2,1)S(1)} %collective-permute-done.13.grid_ref), custom_call_target="tpu_custom_call" | custom-call | flops 134217728 | bytes 4194304 | tf_op jit(solution)/shard_map/backward_end/pallas_call | solution.py:428
  (32 shorter events, 4.1 us)
Async XLA Ops:
  2.6 7.4 %collective-permute-start = (bf16[256,256]{1,0:T(8,128)(2,1)S(1)}, bf16[256,256]{1,0:T(8,128)(2,1)S(1)}, u32[]{:S(2)}, u32[]{:S(2)}) collective-permute-start(bf16[256,256]{1,0:T(8,128)(2,1)S(1)} %forward_chunk.2), channel_id=1, source_target_pairs={{0,8},{8,0},{16,24},{24,16},{1,9},{9,1},{17,25},{25,17},{2,10},{10... | collective-permute-start | bytes 393224 | tf_op jit(solution)/shard_map/ppermute | solution.py:441
  6.0 7.8 %collective-permute-start.1 = (bf16[256,256]{1,0:T(8,128)(2,1)S(1)}, bf16[256,256]{1,0:T(8,128)(2,1)S(1)}, u32[]{:S(2)}, u32[]{:S(2)}) collective-permute-start(bf16[256,256]{1,0:T(8,128)(2,1)S(1)} %forward_chunk.3), channel_id=1, source_target_pairs={{0,16},{8,24},{16,0},{24,8},{1,17},{9,25},{17,1},{25,9},{2,18},{10... | collective-permute-start | bytes 393224 | tf_op jit(solution)/shard_map/ppermute | solution.py:441
  7.6 6.3 %collective-permute-start.2 = (bf16[256,256]{1,0:T(8,128)(2,1)S(1)}, bf16[256,256]{1,0:T(8,128)(2,1)S(1)}, u32[]{:S(2)}, u32[]{:S(2)}) collective-permute-start(bf16[256,256]{1,0:T(8,128)(2,1)S(1)} %get-tuple-element.22), channel_id=1, source_target_pairs={{0,24},{8,16},{16,8},{24,0},{1,25},{9,17},{17,9},{25,1},{2,26},{10... | collective-permute-start | bytes 393224 | tf_op jit(solution)/shard_map/ppermute | solution.py:441
  13.9 4.8 %collective-permute-start.3 = (bf16[64,256]{1,0:T(8,128)(2,1)S(1)}, bf16[64,256]{1,0:T(8,128)(2,1)S(1)}, u32[]{:S(2)}, u32[]{:S(2)}) collective-permute-start(bf16[64,256]{1,0:T(8,128)(2,1)S(1)} %get-tuple-element.25), channel_id=1, source_target_pairs={{0,2},{1,3},{2,0},{3,1},{4,6},{5,7},{6,4},{7,5},{8,10},{9,11},{10,... | collective-permute-start | bytes 98312 | tf_op jit(solution)/shard_map/ppermute | solution.py:441
  15.5 5.4 %collective-permute-start.4 = (bf16[64,256]{1,0:T(8,128)(2,1)S(1)}, bf16[64,256]{1,0:T(8,128)(2,1)S(1)}, u32[]{:S(2)}, u32[]{:S(2)}) collective-permute-start(bf16[64,256]{1,0:T(8,128)(2,1)S(1)} %get-tuple-element.26), channel_id=1, source_target_pairs={{0,4},{1,5},{2,6},{3,7},{4,0},{5,1},{6,2},{7,3},{8,12},{9,13},{10,... | collective-permute-start | bytes 98312 | tf_op jit(solution)/shard_map/ppermute | solution.py:441
  18.1 5.7 %collective-permute-start.5 = (bf16[64,256]{1,0:T(8,128)(2,1)S(1)}, bf16[64,256]{1,0:T(8,128)(2,1)S(1)}, u32[]{:S(2)}, u32[]{:S(2)}) collective-permute-start(bf16[64,256]{1,0:T(8,128)(2,1)S(1)} %get-tuple-element.27), channel_id=1, source_target_pairs={{0,6},{1,7},{2,4},{3,5},{4,2},{5,3},{6,0},{7,1},{8,14},{9,15},{10,... | collective-permute-start | bytes 98312 | tf_op jit(solution)/shard_map/ppermute | solution.py:441
  24.2 1.6 %collective-permute-start.6 = (f32[32,2048]{1,0:T(8,128)S(1)}, f32[32,2048]{1,0:T(8,128)S(1)}, u32[]{:S(2)}, u32[]{:S(2)}) collective-permute-start(f32[32,2048]{1,0:T(8,128)S(1)} %get-tuple-element.29), channel_id=1, source_target_pairs={{0,1},{1,0},{2,3},{3,2},{4,5},{5,4},{6,7},{7,6},{8,9},{9,8},{10,11... | collective-permute-start | bytes 786440 | tf_op jit(solution)/shard_map/ppermute | solution.py:441
  25.8 1.4 %collective-permute-start.7 = (bf16[32,2048]{1,0:T(8,128)(2,1)S(1)}, bf16[32,2048]{1,0:T(8,128)(2,1)S(1)}, u32[]{:S(2)}, u32[]{:S(2)}) collective-permute-start(bf16[32,2048]{1,0:T(8,128)(2,1)S(1)} %act.1.mine_ref), channel_id=1, source_target_pairs={{0,1},{1,0},{2,3},{3,2},{4,5},{5,4},{6,7},{7,6},{8,9},{9,8},{10,11... | collective-permute-start | bytes 393224 | tf_op jit(solution)/shard_map/ppermute | solution.py:441
  28.1 10.8 %copy-start.3 = (f32[1024]{0:T(1024)S(1)}, f32[1024]{0:T(1024)}, u32[]{:S(2)}) copy-start(f32[1024]{0:T(1024)} %param.10) | copy-start | bytes 12292
  28.1 11.0 %copy-start = (bf16[1024,256]{1,0:T(8,128)(2,1)S(1)}, bf16[1024,256]{1,0:T(8,128)(2,1)}, u32[]{:S(2)}) copy-start(bf16[1024,256]{1,0:T(8,128)(2,1)} %coeff_ref.1) | copy-start | bytes 1572868
  28.1 11.0 %copy-start.1 = (s32[16]{0:T(128)S(1)}, s32[16]{0:T(128)}, u32[]{:S(2)}) copy-start(s32[16]{0:T(128)} %pad_ref.3) | copy-start | bytes 196
  28.1 11.0 %copy-start.2 = (f32[256]{0:T(256)S(1)}, f32[256]{0:T(256)}, u32[]{:S(2)}) copy-start(f32[256]{0:T(256)} %param.11) | copy-start | bytes 3076
  28.6 4.9 %collective-permute-start.9 = (bf16[64,256]{1,0:T(8,128)(2,1)S(1)}, bf16[64,256]{1,0:T(8,128)(2,1)S(1)}, u32[]{:S(2)}, u32[]{:S(2)}) collective-permute-start(bf16[64,256]{1,0:T(8,128)(2,1)S(1)} %functions_more.5), channel_id=1, source_target_pairs={{0,4},{1,5},{2,6},{3,7},{4,0},{5,1},{6,2},{7,3},{8,12},{9,13},{10,... | collective-permute-start | bytes 98312 | tf_op jit(solution)/shard_map/ppermute | solution.py:441
  28.7 4.8 %collective-permute-start.8 = (bf16[64,256]{1,0:T(8,128)(2,1)S(1)}, bf16[64,256]{1,0:T(8,128)(2,1)S(1)}, u32[]{:S(2)}, u32[]{:S(2)}) collective-permute-start(bf16[64,256]{1,0:T(8,128)(2,1)S(1)} %functions_more.4), channel_id=1, source_target_pairs={{0,2},{1,3},{2,0},{3,1},{4,6},{5,7},{6,4},{7,5},{8,10},{9,11},{10,... | collective-permute-start | bytes 98312 | tf_op jit(solution)/shard_map/ppermute | solution.py:441
  29.6 5.7 %collective-permute-start.10 = (bf16[64,256]{1,0:T(8,128)(2,1)S(1)}, bf16[64,256]{1,0:T(8,128)(2,1)S(1)}, u32[]{:S(2)}, u32[]{:S(2)}) collective-permute-start(bf16[64,256]{1,0:T(8,128)(2,1)S(1)} %get-tuple-element.32), channel_id=1, source_target_pairs={{0,6},{1,7},{2,4},{3,5},{4,2},{5,3},{6,0},{7,1},{8,14},{9,15},{10,... | collective-permute-start | bytes 98312 | tf_op jit(solution)/shard_map/ppermute | solution.py:441
  35.3 6.1 %collective-permute-start.11 = (bf16[256,256]{1,0:T(8,128)(2,1)S(1)}, bf16[256,256]{1,0:T(8,128)(2,1)}, u32[]{:S(2)}, u32[]{:S(2)}) collective-permute-start(bf16[256,256]{1,0:T(8,128)(2,1)S(1)} %assemble.1.grid_ref), channel_id=1, source_target_pairs={{0,8},{8,0},{16,24},{24,16},{1,9},{9,1},{17,25},{25,17},{2,10},{10... | collective-permute-start | bytes 393224 | tf_op jit(solution)/shard_map/ppermute | solution.py:441
  36.1 6.4 %collective-permute-start.12 = (bf16[256,256]{1,0:T(8,128)(2,1)S(1)}, bf16[256,256]{1,0:T(8,128)(2,1)S(1)}, u32[]{:S(2)}, u32[]{:S(2)}) collective-permute-start(bf16[256,256]{1,0:T(8,128)(2,1)S(1)} %assemble.1.grid_ref), channel_id=1, source_target_pairs={{0,16},{8,24},{16,0},{24,8},{1,17},{9,25},{17,1},{25,9},{2,18},{10... | collective-permute-start | bytes 393224 | tf_op jit(solution)/shard_map/ppermute | solution.py:441
  37.4 6.0 %collective-permute-start.13 = (bf16[256,256]{1,0:T(8,128)(2,1)S(1)}, bf16[256,256]{1,0:T(8,128)(2,1)S(1)}, u32[]{:S(2)}, u32[]{:S(2)}) collective-permute-start(bf16[256,256]{1,0:T(8,128)(2,1)S(1)} %assemble.1.grid_ref), channel_id=1, source_target_pairs={{0,24},{8,16},{16,8},{24,0},{1,25},{9,17},{17,9},{25,1},{2,26},{10... | collective-permute-start | bytes 393224 | tf_op jit(solution)/shard_map/ppermute | solution.py:441

commit v4 on v3

--- a/solution.py
+++ b/solution.py
@@ -50,14 +50,29 @@
     return dot(turned_ref[...], rolled_ref[:, pl.ds(start, own)])
 
 
+def store_halves(chips, total, far_ref, near_ref):
+    upper = lax.axis_index("narrow") // 2 >= chips // 2
+    rows = far_ref.shape[0]
+    turned = total.astype(BF16).T.astype(F32)
+    low, high = turned[:rows], turned[rows:]
+    far_ref[...] = jnp.where(upper, low, high).astype(BF16)
+    near_ref[...] = jnp.where(upper, high, low).astype(BF16)
+
+
+def halves(rows, columns):
+    return (array((rows // 2, columns), BF16),) * 2
+
+
 def first_kernel(
     wide,
+    chips,
     level_hbm,
     pad_hbm,
     shift_hbm,
     coeff_hbm,
     table_hbm,
-    out_ref,
+    far_ref,
+    near_ref,
     turned_ref,
     rolled_ref,
     level_ref,
@@ -83,36 +98,34 @@
     for copy in copies[:4]:
         copy.wait()
     slots = pad_ref.shape[0]
-    width = table_ref.shape[1]
+    width, points = table_ref.shape[1:]
+    row = lax.broadcasted_iota(jnp.int32, (width, 128), 0)
     for s in range(slots):
         rows = slice(s * width, (s + 1) * width)
-        rolled_ref[rows, :] = pltpu.roll(table_ref[level_ref[s]], shift_ref[s], 1)
+        live = jnp.where(row < width - pad_ref[s], 1.0, 0.0).astype(BF16)
+        rolled = pltpu.roll(table_ref[level_ref[s]], shift_ref[s], 1)
+        for p in range(0, points, 128):
+            rolled_ref[rows, p : p + 128] = rolled[:, p : p + 128] * live
     copies[4].wait()
-    row = lax.broadcasted_iota(jnp.int32, (width, coeff_ref.shape[1]), 0)
-    pieces = []
-    for s in range(slots):
-        rows = slice(s * width, (s + 1) * width)
-        piece = coeff_ref[rows, :].astype(F32)
-        pieces.append(jnp.where(row < width - pad_ref[s], piece, 0.0).astype(BF16))
-    turned_ref[...] = jnp.concatenate(pieces, axis=0).T
-    out_ref[...] = chunk_of(turned_ref, rolled_ref, wide, wide - 1).astype(BF16).T
-
-
-def first(wide, level, pad, shift, coeff, tables):
+    turned_ref[...] = coeff_ref[...].T
+    store_halves(chips, chunk_of(turned_ref, rolled_ref, wide, wide - 1), far_ref, near_ref)
+
+
+def first(wide, chips, level, pad, shift, coeff, tables):
     rows, columns = coeff.shape
     points = tables.shape[2]
     slots = pad.shape[0]
     inputs = (level, pad, shift, coeff, tables)
     return call(
-        functools.partial(first_kernel, wide),
+        functools.partial(first_kernel, wide, chips),
         "forward_first",
         (
-            array((points // wide, columns), BF16),
+            *halves(points // wide, columns),
             array((columns, rows), BF16),
             array((rows, points), BF16),
         ),
         [HBM] * 5,
-        (VMEM,) * 3,
+        (VMEM,) * 4,
         [
             pltpu.SMEM((slots,), jnp.int32),
             pltpu.SMEM((slots,), jnp.int32),
@@ -126,19 +139,19 @@
     )(*(in_hbm(value) for value in inputs))
 
 
-def chunk_kernel(wide, k, turned_ref, rolled_ref, out_ref):
-    out_ref[...] = chunk_of(turned_ref, rolled_ref, wide, k).astype(BF16).T
-
-
-def chunk(wide, k, turned, rolled):
+def chunk_kernel(wide, chips, k, turned_ref, rolled_ref, far_ref, near_ref):
+    store_halves(chips, chunk_of(turned_ref, rolled_ref, wide, k), far_ref, near_ref)
+
+
+def chunk(wide, chips, k, turned, rolled):
     columns, rows = turned.shape
     own = rolled.shape[1] // wide
     return call(
-        functools.partial(chunk_kernel, wide, k),
+        functools.partial(chunk_kernel, wide, chips, k),
         "forward_chunk",
-        array((own, columns), BF16),
+        halves(own, columns),
         [VMEM] * 2,
-        VMEM,
+        (VMEM,) * 2,
         flops=2 * rows * own * columns * LONG,
         moved=MIB * LONG,
     )(turned, rolled)
@@ -194,29 +207,31 @@
     )(turned, rolled, in_hbm(basis), in_hbm(potential))
 
 
-def combine_kernel(wide, chips, *refs):
-    parts, outs = refs[:wide], refs[wide:]
+def combine_kernel(chips, first, mine_ref, *refs):
+    count = chips // 2
+    parts, outs = refs[:-count], refs[-count:]
     chip = lax.axis_index("narrow") // 2
     rows = outs[0].shape[0]
-    for j in range(chips):
-        start = pl.multiple_of((chip ^ j) * rows, rows)
-        total = parts[0][pl.ds(start, rows), :]
-        for part in parts[1:]:
+    for i in range(count):
+        target = chip ^ (first + i)
+        total = mine_ref[pl.ds(pl.multiple_of(target * rows, rows), rows), :]
+        start = pl.multiple_of((target % count) * rows, rows)
+        for part in parts:
             total = total + part[pl.ds(start, rows), :].astype(F32)
-        outs[j][...] = total.astype(BF16)
-
-
-def combine(chips, parts):
-    rows, columns = parts[0].shape
-    wide = len(parts)
-    return call(
-        functools.partial(combine_kernel, wide, chips),
+        outs[i][...] = total.astype(BF16)
+
+
+def combine(chips, first, mine, parts):
+    rows, columns = mine.shape
+    count = chips // 2
+    return call(
+        functools.partial(combine_kernel, chips, first),
         "wide_sum",
-        tuple(array((rows // chips, columns), BF16) for _ in range(chips)),
-        [VMEM] * wide,
-        (VMEM,) * chips,
+        (array((rows // chips, columns), BF16),) * count,
+        [VMEM] * (len(parts) + 1),
+        (VMEM,) * count,
         moved=MIB,
-    )(*parts)
+    )(mine, *parts)
 
 
 def own_points_kernel(x_ref, basis_ref, out_ref):
@@ -330,111 +345,123 @@
     )(both, basis)
 
 
-def assemble_kernel(*refs):
+def assemble_kernel(first, *refs):
     parts, out_ref = refs[:-1], refs[-1]
     chip = lax.axis_index("narrow") // 2
     rows = parts[0].shape[0]
-    for j, part in enumerate(parts):
-        start = pl.multiple_of((chip ^ j) * rows, rows)
-        out_ref[pl.ds(start, rows), :] = part[...]
-
-
-def assemble(parts):
+    for i, part in enumerate(parts):
+        place = (chip ^ (first + i)) % len(parts)
+        out_ref[pl.ds(pl.multiple_of(place * rows, rows), rows), :] = part[...]
+
+
+def assemble(first, parts):
     rows, columns = parts[0].shape
-    chips = len(parts)
-    return call(
-        assemble_kernel,
+    count = len(parts)
+    return call(
+        functools.partial(assemble_kernel, first),
         "assemble",
-        array((rows * chips, columns), BF16),
-        [VMEM] * chips,
+        array((rows * count, columns), BF16),
+        [VMEM] * count,
         VMEM,
         moved=MIB // 4,
     )(*parts)
 
 
-def own_kernel(wide, pad_ref, rolled_ref, grid_ref, coeff_ref, row_ref, column_ref, out_ref):
+def columns_of(chips, wide, k, far, half):
+    upper = lax.axis_index("narrow") // 2 // (chips // 2)
+    place = (lax.axis_index("wide") ^ k) * 2 + (upper ^ far)
+    return pl.ds(pl.multiple_of(place * half, half), half)
+
+
+def own_kernel(wide, chips, pad_ref, rolled_ref, near_ref, coeff_ref, row_ref, column_ref, out_ref):
     slots = pad_ref.shape[0]
     width = rolled_ref.shape[0] // slots
-    me = lax.axis_index("wide")
-    own = rolled_ref.shape[1] // wide
-    start = pl.multiple_of(me * own, own)
-    out_ref[...] = dot(rolled_ref[:, pl.ds(start, own)], grid_ref[...])
-    for s in range(slots):
-        rows = slice(s * width, (s + 1) * width)
+    half = near_ref.shape[0]
+    mine = columns_of(chips, wide, 0, 0, half)
+    row = lax.broadcasted_iota(jnp.int32, (width, out_ref.shape[1]), 0)
+
+    def one(s, _):
+        rows = pl.ds(pl.multiple_of(s * width, width), width)
         energy = row_ref[rows, :] + column_ref[...]
-        out_ref[rows, :] += energy * coeff_ref[rows, :].astype(F32)
-
-
-def backward_own(wide, pad, rolled, grid, coeff, row_energy, column_energy):
+        diagonal = energy * coeff_ref[rows, :].astype(F32)
+        diagonal = jnp.where(row < width - pad_ref[s], diagonal, 0.0)
+        out_ref[rows, :] = diagonal + dot(rolled_ref[rows, mine], near_ref[...])
+        return 0
+
+    lax.fori_loop(0, slots, one, 0, unroll=4)
+
+
+def backward_own(wide, chips, pad, rolled, near, coeff, row_energy, column_energy):
     smem = pl.BlockSpec(memory_space=pltpu.SMEM)
     rows, columns = coeff.shape
     return call(
-        functools.partial(own_kernel, wide),
+        functools.partial(own_kernel, wide, chips),
         "backward_own",
         array(coeff.shape, F32),
         [smem] + [VMEM] * 5,
         VMEM,
-        flops=2 * rows * columns * rolled.shape[1] // wide,
+        flops=2 * rows * columns * near.shape[0],
         moved=4 * MIB,
-    )(pad, rolled, grid, coeff, row_energy[:, None], column_energy[None, :])
-
-
-def more_kernel(wide, k, total_ref, rolled_ref, grid_ref, out_ref):
-    own = rolled_ref.shape[1] // wide
-    start = pl.multiple_of((lax.axis_index("wide") ^ k) * own, own)
-    out_ref[...] = total_ref[...] + dot(rolled_ref[:, pl.ds(start, own)], grid_ref[...])
-
-
-def backward_more(wide, k, total, rolled, grid):
+    )(pad, rolled, near, coeff, row_energy[:, None], column_energy[None, :])
+
+
+def more_kernel(wide, chips, pieces, total_ref, rolled_ref, *refs):
+    grids, out_ref = refs[:-1], refs[-1]
+    half = grids[0].shape[0]
+    steps = 4
+    count = rolled_ref.shape[0] // steps
+
+    def one(i, _):
+        rows = pl.ds(pl.multiple_of(i * count, count), count)
+        total = total_ref[rows, :]
+        for (k, far), grid in zip(pieces, grids):
+            place = columns_of(chips, wide, k, far, half)
+            total = total + dot(rolled_ref[rows, place], grid[...])
+        out_ref[rows, :] = total
+        return 0
+
+    lax.fori_loop(0, steps, one, 0)
+
+
+def backward_more(wide, chips, pieces, total, rolled, grids):
     rows, columns = total.shape
     return call(
-        functools.partial(more_kernel, wide, k),
+        functools.partial(more_kernel, wide, chips, pieces),
         "backward_more",
         array(total.shape, F32),
-        [VMEM] * 3,
+        [VMEM] * (2 + len(grids)),
         VMEM,
-        flops=2 * rows * columns * rolled.shape[1] // wide,
+        flops=2 * rows * columns * grids[0].shape[0] * len(grids),
         moved=3 * MIB,
-    )(total, rolled, grid)
-
-
-def end_kernel(wide, k, pad_ref, total_ref, rolled_ref, grid_ref, out_hbm, out_ref, sems):
-    slots = pad_ref.shape[0]
-    width = rolled_ref.shape[0] // slots
-    own = rolled_ref.shape[1] // wide
-    start = pl.multiple_of((lax.axis_index("wide") ^ k) * own, own)
+    )(total, rolled, *grids)
+
+
+def end_kernel(wide, chips, k, far, total_ref, rolled_ref, grid_ref, out_hbm, out_ref, sems):
+    place = columns_of(chips, wide, k, far, grid_ref.shape[0])
     steps = sems.shape[0]
     rows = rolled_ref.shape[0] // steps
-    row = lax.broadcasted_iota(jnp.int32, (width, out_ref.shape[1]), 0)
     copies = []
     for i in range(steps):
         span = pl.ds(i * rows, rows)
-        total = total_ref[span, :] + dot(rolled_ref[span, pl.ds(start, own)], grid_ref[...])
-        for s in range(rows // width):
-            slot = i * (rows // width) + s
-            value = total[s * width : (s + 1) * width, :]
-            out_ref[pl.ds(slot * width, width), :] = jnp.where(
-                row < width - pad_ref[slot], value, 0.0
-            )
+        out_ref[span, :] = total_ref[span, :] + dot(rolled_ref[span, place], grid_ref[...])
         copies.append(pltpu.make_async_copy(out_ref.at[span, :], out_hbm.at[span, :], sems.at[i]))
         copies[-1].start()
     for copy in copies:
         copy.wait()
 
 
-def backward_end(wide, k, pad, total, rolled, grid):
-    smem = pl.BlockSpec(memory_space=pltpu.SMEM)
+def backward_end(wide, chips, k, far, total, rolled, grid):
     rows, columns = total.shape
     return call(
-        functools.partial(end_kernel, wide, k),
+        functools.partial(end_kernel, wide, chips, k, far),
         "backward_end",
         array(total.shape, F32),
-        [smem] + [VMEM] * 3,
+        [VMEM] * 3,
         HBM,
         [pltpu.VMEM(total.shape, F32), pltpu.SemaphoreType.DMA((4,))],
-        flops=2 * rows * columns * rolled.shape[1] // wide,
+        flops=2 * rows * columns * grid.shape[0],
         moved=4 * MIB,
-    )(pad, total, rolled, grid)
+    )(total, rolled, grid)
 
 
 def exchange(value, step, size, axis):
@@ -456,33 +483,48 @@
 ):
     chips = narrow // 2
     tables = jnp.swapaxes(groupb_basis_values, 1, 2)
-    far, turned, rolled = first(
-        wide, slot_sparse_level, block_pad, slot_grid_offset, coeff, tables
+    half = chips // 2
+    order = [wide - 1] + list(range(1, wide - 1))
+    far, near, turned, rolled = first(
+        wide, chips, slot_sparse_level, block_pad, slot_grid_offset, coeff, tables
     )
-    arrived = {wide - 1: exchange(far, wide - 1, wide, "wide")}
-    for k in range(1, wide - 1):
-        arrived[k] = exchange(chunk(wide, k, turned, rolled), k, wide, "wide")
+    sent = {wide - 1: (far, near)}
+    for k in order[1:]:
+        sent[k] = chunk(wide, chips, k, turned, rolled)
+    far_parts = [exchange(sent[k][0], k, wide, "wide") for k in order]
+    near_parts = [exchange(sent[k][1], k, wide, "wide") for k in order]
     mine, basis, pot = last(wide, chips, turned, rolled, basis_a, potential)
-    pieces = combine(chips, [mine] + [arrived[k] for k in range(1, wide)])
-    xs = [exchange(pieces[j], 2 * j, narrow, "narrow") for j in range(1, chips)]
+    pieces = combine(chips, half, mine, far_parts)
+    xs = {j: exchange(pieces[j - half], 2 * j, narrow, "narrow") for j in range(half, chips)}
+    pieces = combine(chips, 0, mine, near_parts)
+    for j in range(1, half):
+        xs[j] = exchange(pieces[j], 2 * j, narrow, "narrow")
     total = own_points(pieces[0], basis)
-    for j in range(1, chips - 1):
-        total = more_points(j, total, xs[j - 1], basis)
-    mine, theirs = last_points(chips - 1, total, xs[-1], basis)
+    visits = list(range(half, chips)) + list(range(1, half))
+    for j in visits[:-1]:
+        total = more_points(j, total, xs[j], basis)
+    mine, theirs = last_points(visits[-1], total, xs[visits[-1]], basis)
     acted = act(mine, exchange(theirs, 1, narrow, "narrow"), pot)
     other = exchange(acted, 1, narrow, "narrow")
-    block, both = first_functions(chips - 1, acted, other, basis)
-    sent = {chips - 1: exchange(block, 2 * (chips - 1), narrow, "narrow")}
-    for j in reversed(range(1, chips - 1)):
-        sent[j] = exchange(functions(j, both, basis), 2 * j, narrow, "narrow")
-    grid = assemble([functions(0, both, basis)] + [sent[j] for j in range(1, chips)])
-    grids = [exchange(grid, k, wide, "wide") for k in range(1, wide)]
+    blocks = {}
+    block, both = first_functions(1, acted, other, basis)
+    blocks[1] = exchange(block, 2, narrow, "narrow")
+    for j in range(2, chips):
+        blocks[j] = exchange(functions(j, both, basis), 2 * j, narrow, "narrow")
+    near = assemble(0, [functions(0, both, basis)] + [blocks[j] for j in range(1, half)])
+    nears = [exchange(near, k, wide, "wide") for k in order]
+    far = assemble(half, [blocks[j] for j in range(half, chips)])
+    fars = [exchange(far, k, wide, "wide") for k in order]
     total = backward_own(
-        wide, block_pad, rolled, grid, coeff, groupb_row_energy, groupa_energy
+        wide, chips, block_pad, rolled, near, coeff, groupb_row_energy, groupa_energy
     )
-    for k in range(1, wide - 1):
-        total = backward_more(wide, k, total, rolled, grids[k - 1])
-    return backward_end(wide, wide - 1, block_pad, total, rolled, grids[-1])
+    total = backward_more(
+        wide, chips, [(0, 1)] + [(k, 0) for k in order], total, rolled, [far] + nears
+    )
+    total = backward_more(
+        wide, chips, [(k, 1) for k in order[:-1]], total, rolled, fars[:-1]
+    )
+    return backward_end(wide, chips, order[-1], 1, total, rolled, fars[-1])
 
 
 def solution(mesh):

time: 45.3 us -> 50.7 us (1.12)
  starting transfers between devices: 17.4 us -> 22.2 us
  Pallas kernels: 12.5 us -> 14.8 us
  waiting for transfers between devices: 14.8 us -> 12.9 us
    ppermute x14 -> x20, starting transfers between devices: 17.4 us -> 22.2 us  [exchange(): return lax.ppermute(value, axis, [(i, i ^ step) for i in range(size)])]
    pallas_call x9 -> x11, Pallas kernels: 7.16 us -> 9.44 us  [the longest x2 2.93 us: backward_more(): call(functools.partial(more_kernel, wide, chips, pieces), 'backward_more'...]
    ppermute x14 -> x20, waiting for transfers between devices: 14.8 us -> 12.9 us  [exchange(): return lax.ppermute(value, axis, [(i, i ^ step) for i in range(size)])]
  transfers between devices with their start and end apart: 14 -> 20, of which waited for: 8 -> 7; matrix products, arithmetic and copies ran while one was open for 0% -> 0% of each run, Pallas kernels for 14% -> 18%
where the time goes in v4:
time: 50.7 us; the launch traced here: 50.5 us
  starting transfers between devices  22.2 us (44%)
  Pallas kernels  14.8 us (29%)
  waiting for transfers between devices  12.9 us (25%)
    ppermute x20, starting transfers between devices, exchange(): return lax.ppermute(value, axis, [(i, i ^ step) for i in range(size)])  22.2 us
    ppermute x20, waiting for transfers between devices, exchange(): return lax.ppermute(value, axis, [(i, i ^ step) for i in range(size)])  12.9 us
    pallas_call x2, Pallas kernels, backward_more(): call(functools.partial(more_kernel, wide, chips, pieces), 'backward_more'...  2.93 us
    pallas_call x1, Pallas kernels, last(): call(functools.partial(last_kernel, wide, chips), 'forward_own', (array((...  2.39 us
    pallas_call x1, Pallas kernels, first(): call(functools.partial(first_kernel, wide, chips), 'forward_first', (*hal...  2.26 us
    pallas_call x1, Pallas kernels, backward_end(): call(functools.partial(end_kernel, wide, chips, k, far), 'backward_end',...  2.06 us
    pallas_call x3, Pallas kernels, functions(): call(functools.partial(functions_kernel, j), 'functions_more', array((row...  1.33 us
    pallas_call x1, Pallas kernels, backward_own(): call(functools.partial(own_kernel, wide, chips), 'backward_own', array(co...  1.31 us
  transfers between devices with their start and end apart: 20, of which 7 were waited for; matrix products, arithmetic and copies ran while one was open for 0% of the time, Pallas kernels for 18%

profile of v4, /device:TPU:0, one launch (start us, length us, event | category | flops | bytes accessed | tf_op | source)
XLA Modules:
  0.0 50.5 jit_solution(3117476961181887454)
XLA Ops:
  0.0 2.3 %forward_first.1 = (bf16[128,256]{1,0:T(8,128)(2,1)S(1)}, bf16[128,256]{1,0:T(8,128)(2,1)S(1)}, bf16[256,1024]{1,0:T(8,128)(2,1)S(1)}, bf16[1024,1024]{1,0:T(8,128)(2,1)S(1)}) custom-call(s32[16]{0:T(128)} %level_hbm.1, s32[16]{0:T(128)} %pad_ref.1, s32[16]{0:T(128)} %shift_hbm.1, bf16[1024,256]{1,0:T(8,128)(2,1)} %coeff_ref.1, bf16[4,64,1024]{2,1,0:T(8,128)(2,1)} %bitcast.4), custom_call_target="tpu_custom_call" | custom-call | flops 134217728 | bytes 4194304 | tf_op jit(solution)/shard_map/forward_first/pallas_call | solution.py:119
  2.7 3.0 %collective-permute-start.4 = (bf16[128,256]{1,0:T(8,128)(2,1)S(1)}, bf16[128,256]{1,0:T(8,128)(2,1)S(1)}, u32[]{:S(2)}, u32[]{:S(2)}) collective-permute-start(bf16[128,256]{1,0:T(8,128)(2,1)S(1)} %get-tuple-element.33), channel_id=1, source_target_pairs={{0,8},{8,0},{16,24},{24,16},{1,9},{9,1},{17,25},{25,17},{2,10},{10... | collective-permute-start | bytes 196616 | tf_op jit(solution)/shard_map/ppermute | solution.py:468
  6.0 1.6 %collective-permute-start.5 = (bf16[128,256]{1,0:T(8,128)(2,1)S(1)}, bf16[128,256]{1,0:T(8,128)(2,1)S(1)}, u32[]{:S(2)}, u32[]{:S(2)}) collective-permute-start(bf16[128,256]{1,0:T(8,128)(2,1)S(1)} %get-tuple-element.34), channel_id=1, source_target_pairs={{0,16},{8,24},{16,0},{24,8},{1,17},{9,25},{17,1},{25,9},{2,18},{10... | collective-permute-start | bytes 196616 | tf_op jit(solution)/shard_map/ppermute | solution.py:468
  7.7 1.9 %collective-permute-start.1 = (bf16[128,256]{1,0:T(8,128)(2,1)S(1)}, bf16[128,256]{1,0:T(8,128)(2,1)S(1)}, u32[]{:S(2)}, u32[]{:S(2)}) collective-permute-start(bf16[128,256]{1,0:T(8,128)(2,1)S(1)} %get-tuple-element.28), channel_id=1, source_target_pairs={{0,8},{8,0},{16,24},{24,16},{1,9},{9,1},{17,25},{25,17},{2,10},{10... | collective-permute-start | bytes 196616 | tf_op jit(solution)/shard_map/ppermute | solution.py:468
  9.6 1.5 %collective-permute-start.2 = (bf16[128,256]{1,0:T(8,128)(2,1)S(1)}, bf16[128,256]{1,0:T(8,128)(2,1)S(1)}, u32[]{:S(2)}, u32[]{:S(2)}) collective-permute-start(bf16[128,256]{1,0:T(8,128)(2,1)S(1)} %get-tuple-element.29), channel_id=1, source_target_pairs={{0,16},{8,24},{16,0},{24,8},{1,17},{9,25},{17,1},{25,9},{2,18},{10... | collective-permute-start | bytes 196616 | tf_op jit(solution)/shard_map/ppermute | solution.py:468
  11.2 2.4 %forward_own.1 = (f32[256,256]{1,0:T(8,128)S(1)}, bf16[4,256,2048]{2,1,0:T(8,128)(2,1)S(1)}, f32[32,2048]{1,0:T(8,128)S(1)}) custom-call(bf16[256,1024]{1,0:T(8,128)(2,1)S(1)} %get-tuple-element.25.turned_ref, bf16[1024,1024]{1,0:T(8,128)(2,1)S(1)} %get-tuple-element.24.rolled_ref, bf16[2048,2048]{1,0:T(8,128)(2,1)} %basis_hbm.1, f32[32,2048]{1,0:T(8,128)} %potential_hbm.1), custom_call_target="tpu_custom_call" | custom-call | flops 134217728 | bytes 10485760 | tf_op jit(solution)/shard_map/forward_own/pallas_call | solution.py:194
  13.7 3.1 %collective-permute-start.6 = (bf16[64,256]{1,0:T(8,128)(2,1)S(1)}, bf16[64,256]{1,0:T(8,128)(2,1)S(1)}, u32[]{:S(2)}, u32[]{:S(2)}) collective-permute-start(bf16[64,256]{1,0:T(8,128)(2,1)S(1)} %get-tuple-element.35), channel_id=1, source_target_pairs={{0,4},{1,5},{2,6},{3,7},{4,0},{5,1},{6,2},{7,3},{8,12},{9,13},{10,... | collective-permute-start | bytes 98312 | tf_op jit(solution)/shard_map/ppermute | solution.py:468
  16.7 1.3 %collective-permute-start.7 = (bf16[64,256]{1,0:T(8,128)(2,1)S(1)}, bf16[64,256]{1,0:T(8,128)(2,1)S(1)}, u32[]{:S(2)}, u32[]{:S(2)}) collective-permute-start(bf16[64,256]{1,0:T(8,128)(2,1)S(1)} %get-tuple-element.36), channel_id=1, source_target_pairs={{0,6},{1,7},{2,4},{3,5},{4,2},{5,3},{6,0},{7,1},{8,14},{9,15},{10,... | collective-permute-start | bytes 98312 | tf_op jit(solution)/shard_map/ppermute | solution.py:468
  19.3 3.2 %collective-permute-done.7.x_ref = bf16[64,256]{1,0:T(8,128)(2,1)S(1)} collective-permute-done((bf16[64,256]{1,0:T(8,128)(2,1)S(1)}, bf16[64,256]{1,0:T(8,128)(2,1)S(1)}, u32[]{:S(2)}, u32[]{:S(2)}) %collective-permute-start.7) | collective-permute-done | bytes 32800 | tf_op jit(solution)/shard_map/ppermute | solution.py:468
  23.2 1.5 %collective-permute-done.9.other_ref = f32[32,2048]{1,0:T(8,128)S(1)} collective-permute-done((f32[32,2048]{1,0:T(8,128)S(1)}, f32[32,2048]{1,0:T(8,128)S(1)}, u32[]{:S(2)}, u32[]{:S(2)}) %collective-permute-start.9) | collective-permute-done | bytes 262176 | tf_op jit(solution)/shard_map/ppermute | solution.py:468
  25.0 1.2 %collective-permute-done.10.other_ref = bf16[32,2048]{1,0:T(8,128)(2,1)S(1)} collective-permute-done((bf16[32,2048]{1,0:T(8,128)(2,1)S(1)}, bf16[32,2048]{1,0:T(8,128)(2,1)S(1)}, u32[]{:S(2)}, u32[]{:S(2)}) %collective-permute-start.10) | collective-permute-done | bytes 131104 | tf_op jit(solution)/shard_map/ppermute | solution.py:468
  27.6 3.0 %collective-permute-done.11.refs_1_ = bf16[64,256]{1,0:T(8,128)(2,1)S(1)} collective-permute-done((bf16[64,256]{1,0:T(8,128)(2,1)S(1)}, bf16[64,256]{1,0:T(8,128)(2,1)S(1)}, u32[]{:S(2)}, u32[]{:S(2)}) %collective-permute-start.11) | collective-permute-done | bytes 32800 | tf_op jit(solution)/shard_map/ppermute | solution.py:468
  30.6 2.5 %collective-permute-start.14 = (bf16[128,256]{1,0:T(8,128)(2,1)S(1)}, bf16[128,256]{1,0:T(8,128)(2,1)S(1)}, u32[]{:S(2)}, u32[]{:S(2)}) collective-permute-start(bf16[128,256]{1,0:T(8,128)(2,1)S(1)} %assemble.2.near_ref), channel_id=1, source_target_pairs={{0,24},{8,16},{16,8},{24,0},{1,25},{9,17},{17,9},{25,1},{2,26},{10... | collective-permute-start | bytes 196616 | tf_op jit(solution)/shard_map/ppermute | solution.py:468
  33.6 1.9 %collective-permute-start.13 = (bf16[64,256]{1,0:T(8,128)(2,1)S(1)}, bf16[64,256]{1,0:T(8,128)(2,1)S(1)}, u32[]{:S(2)}, u32[]{:S(2)}) collective-permute-start(bf16[64,256]{1,0:T(8,128)(2,1)S(1)} %functions_more.5), channel_id=1, source_target_pairs={{0,6},{1,7},{2,4},{3,5},{4,2},{5,3},{6,0},{7,1},{8,14},{9,15},{10,... | collective-permute-start | bytes 98312 | tf_op jit(solution)/shard_map/ppermute | solution.py:468
  35.4 0.5 %collective-permute-start.15 = (bf16[128,256]{1,0:T(8,128)(2,1)S(1)}, bf16[128,256]{1,0:T(8,128)(2,1)S(1)}, u32[]{:S(2)}, u32[]{:S(2)}) collective-permute-start(bf16[128,256]{1,0:T(8,128)(2,1)S(1)} %assemble.2.near_ref), channel_id=1, source_target_pairs={{0,8},{8,0},{16,24},{24,16},{1,9},{9,1},{17,25},{25,17},{2,10},{10... | collective-permute-start | bytes 196616 | tf_op jit(solution)/shard_map/ppermute | solution.py:468
  36.5 2.9 %collective-permute-done.13.refs_1_ = bf16[64,256]{1,0:T(8,128)(2,1)S(1)} collective-permute-done((bf16[64,256]{1,0:T(8,128)(2,1)S(1)}, bf16[64,256]{1,0:T(8,128)(2,1)S(1)}, u32[]{:S(2)}, u32[]{:S(2)}) %collective-permute-start.13) | collective-permute-done | bytes 32800 | tf_op jit(solution)/shard_map/ppermute | solution.py:468
  39.3 0.9 %collective-permute-done.12.refs_0_ = bf16[64,256]{1,0:T(8,128)(2,1)S(1)} collective-permute-done((bf16[64,256]{1,0:T(8,128)(2,1)S(1)}, bf16[64,256]{1,0:T(8,128)(2,1)S(1)}, u32[]{:S(2)}, u32[]{:S(2)}) %collective-permute-start.12) | collective-permute-done | bytes 32800 | tf_op jit(solution)/shard_map/ppermute | solution.py:468
  40.3 0.5 %collective-permute-start.17 = (bf16[128,256]{1,0:T(8,128)(2,1)S(1)}, bf16[128,256]{1,0:T(8,128)(2,1)S(1)}, u32[]{:S(2)}, u32[]{:S(2)}) collective-permute-start(bf16[128,256]{1,0:T(8,128)(2,1)S(1)} %assemble.3.refs_0_), channel_id=1, source_target_pairs={{0,24},{8,16},{16,8},{24,0},{1,25},{9,17},{17,9},{25,1},{2,26},{10... | collective-permute-start | bytes 196616 | tf_op jit(solution)/shard_map/ppermute | solution.py:468
  40.8 1.5 %collective-permute-start.18 = (bf16[128,256]{1,0:T(8,128)(2,1)S(1)}, bf16[128,256]{1,0:T(8,128)(2,1)}, u32[]{:S(2)}, u32[]{:S(2)}) collective-permute-start(bf16[128,256]{1,0:T(8,128)(2,1)S(1)} %assemble.3.refs_0_), channel_id=1, source_target_pairs={{0,8},{8,0},{16,24},{24,16},{1,9},{9,1},{17,25},{25,17},{2,10},{10... | collective-permute-start | bytes 196616 | tf_op jit(solution)/shard_map/ppermute | solution.py:468
  42.3 1.5 %collective-permute-start.19 = (bf16[128,256]{1,0:T(8,128)(2,1)S(1)}, bf16[128,256]{1,0:T(8,128)(2,1)}, u32[]{:S(2)}, u32[]{:S(2)}) collective-permute-start(bf16[128,256]{1,0:T(8,128)(2,1)S(1)} %assemble.3.refs_0_), channel_id=1, source_target_pairs={{0,16},{8,24},{16,0},{24,8},{1,17},{9,25},{17,1},{25,9},{2,18},{10... | collective-permute-start | bytes 196616 | tf_op jit(solution)/shard_map/ppermute | solution.py:468
  44.1 1.3 %backward_own.1.total_ref = f32[1024,256]{1,0:T(8,128)S(1)} custom-call(s32[16]{0:T(128)S(1)} %copy-done.1, bf16[1024,1024]{1,0:T(8,128)(2,1)S(1)} %get-tuple-element.24.rolled_ref, bf16[128,256]{1,0:T(8,128)(2,1)S(1)} %assemble.2.near_ref, bf16[1024,256]{1,0:T(8,128)(2,1)S(1)} %copy-done, f32[1024,1]{1,0:T(8,128)S(1)} %copy.10.row_ref, f32[1,256]{1,0:T(1,128)S(1)} %bitcast.3), custom_call_target="tpu_custom_call" | custom-call | flops 67108864 | bytes 4194304 | tf_op jit(solution)/shard_map/backward_own/pallas_call | solution.py:397
  45.4 1.2 %backward_more.2.total_ref = f32[1024,256]{1,0:T(8,128)S(1)} custom-call(f32[1024,256]{1,0:T(8,128)S(1)} %backward_own.1.total_ref, bf16[1024,1024]{1,0:T(8,128)(2,1)S(1)} %get-tuple-element.24.rolled_ref, bf16[128,256]{1,0:T(8,128)(2,1)S(1)} %assemble.3.refs_0_, bf16[128,256]{1,0:T(8,128)(2,1)S(1)} %collective-permute-done.14.refs_1_, ...), custom_call_target="tpu_custom_call" | custom-call | flops 268435456 | bytes 3145728 | tf_op jit(solution)/shard_map/backward_more/pallas_call | solution.py:428
  46.6 1.7 %backward_more.3.total_ref = f32[1024,256]{1,0:T(8,128)S(1)} custom-call(f32[1024,256]{1,0:T(8,128)S(1)} %backward_more.2.total_ref, bf16[1024,1024]{1,0:T(8,128)(2,1)S(1)} %get-tuple-element.24.rolled_ref, bf16[128,256]{1,0:T(8,128)(2,1)S(1)} %collective-permute-done.17.refs_0_, bf16[128,256]{1,0:T(8,128)(2,1)} %collective-permute-done.18.refs_1_), custom_call_target="tpu_custom_call" | custom-call | flops 134217728 | bytes 3145728 | tf_op jit(solution)/shard_map/backward_more/pallas_call | solution.py:428
  48.4 2.1 %backward_end.1 = f32[1024,256]{1,0:T(8,128)} custom-call(f32[1024,256]{1,0:T(8,128)S(1)} %backward_more.3.total_ref, bf16[1024,1024]{1,0:T(8,128)(2,1)S(1)} %get-tuple-element.24.rolled_ref, bf16[128,256]{1,0:T(8,128)(2,1)} %collective-permute-done.19.grid_ref), custom_call_target="tpu_custom_call" | custom-call | flops 67108864 | bytes 4194304 | tf_op jit(solution)/shard_map/backward_end/pallas_call | solution.py:455
  (46 shorter events, 5.7 us)
Async XLA Ops:
  2.7 8.5 %collective-permute-start.4 = (bf16[128,256]{1,0:T(8,128)(2,1)S(1)}, bf16[128,256]{1,0:T(8,128)(2,1)S(1)}, u32[]{:S(2)}, u32[]{:S(2)}) collective-permute-start(bf16[128,256]{1,0:T(8,128)(2,1)S(1)} %get-tuple-element.33), channel_id=1, source_target_pairs={{0,8},{8,0},{16,24},{24,16},{1,9},{9,1},{17,25},{25,17},{2,10},{10... | collective-permute-start | bytes 196616 | tf_op jit(solution)/shard_map/ppermute | solution.py:468
  6.0 7.5 %collective-permute-start.5 = (bf16[128,256]{1,0:T(8,128)(2,1)S(1)}, bf16[128,256]{1,0:T(8,128)(2,1)S(1)}, u32[]{:S(2)}, u32[]{:S(2)}) collective-permute-start(bf16[128,256]{1,0:T(8,128)(2,1)S(1)} %get-tuple-element.34), channel_id=1, source_target_pairs={{0,16},{8,24},{16,0},{24,8},{1,17},{9,25},{17,1},{25,9},{2,18},{10... | collective-permute-start | bytes 196616 | tf_op jit(solution)/shard_map/ppermute | solution.py:468
  7.6 6.0 %collective-permute-start.3 = (bf16[128,256]{1,0:T(8,128)(2,1)S(1)}, bf16[128,256]{1,0:T(8,128)(2,1)S(1)}, u32[]{:S(2)}, u32[]{:S(2)}) collective-permute-start(bf16[128,256]{1,0:T(8,128)(2,1)S(1)} %get-tuple-element.32), channel_id=1, source_target_pairs={{0,24},{8,16},{16,8},{24,0},{1,25},{9,17},{17,9},{25,1},{2,26},{10... | collective-permute-start | bytes 196616 | tf_op jit(solution)/shard_map/ppermute | solution.py:468
  7.7 10.4 %collective-permute-start.1 = (bf16[128,256]{1,0:T(8,128)(2,1)S(1)}, bf16[128,256]{1,0:T(8,128)(2,1)S(1)}, u32[]{:S(2)}, u32[]{:S(2)}) collective-permute-start(bf16[128,256]{1,0:T(8,128)(2,1)S(1)} %get-tuple-element.28), channel_id=1, source_target_pairs={{0,8},{8,0},{16,24},{24,16},{1,9},{9,1},{17,25},{25,17},{2,10},{10... | collective-permute-start | bytes 196616 | tf_op jit(solution)/shard_map/ppermute | solution.py:468
  9.6 8.5 %collective-permute-start.2 = (bf16[128,256]{1,0:T(8,128)(2,1)S(1)}, bf16[128,256]{1,0:T(8,128)(2,1)S(1)}, u32[]{:S(2)}, u32[]{:S(2)}) collective-permute-start(bf16[128,256]{1,0:T(8,128)(2,1)S(1)} %get-tuple-element.29), channel_id=1, source_target_pairs={{0,16},{8,24},{16,0},{24,8},{1,17},{9,25},{17,1},{25,9},{2,18},{10... | collective-permute-start | bytes 196616 | tf_op jit(solution)/shard_map/ppermute | solution.py:468
  11.1 7.0 %collective-permute-start = (bf16[128,256]{1,0:T(8,128)(2,1)S(1)}, bf16[128,256]{1,0:T(8,128)(2,1)S(1)}, u32[]{:S(2)}, u32[]{:S(2)}) collective-permute-start(bf16[128,256]{1,0:T(8,128)(2,1)S(1)} %get-tuple-element.27), channel_id=1, source_target_pairs={{0,24},{8,16},{16,8},{24,0},{1,25},{9,17},{17,9},{25,1},{2,26},{10... | collective-permute-start | bytes 196616 | tf_op jit(solution)/shard_map/ppermute | solution.py:468
  13.7 5.4 %collective-permute-start.6 = (bf16[64,256]{1,0:T(8,128)(2,1)S(1)}, bf16[64,256]{1,0:T(8,128)(2,1)S(1)}, u32[]{:S(2)}, u32[]{:S(2)}) collective-permute-start(bf16[64,256]{1,0:T(8,128)(2,1)S(1)} %get-tuple-element.35), channel_id=1, source_target_pairs={{0,4},{1,5},{2,6},{3,7},{4,0},{5,1},{6,2},{7,3},{8,12},{9,13},{10,... | collective-permute-start | bytes 98312 | tf_op jit(solution)/shard_map/ppermute | solution.py:468
  16.7 5.8 %collective-permute-start.7 = (bf16[64,256]{1,0:T(8,128)(2,1)S(1)}, bf16[64,256]{1,0:T(8,128)(2,1)S(1)}, u32[]{:S(2)}, u32[]{:S(2)}) collective-permute-start(bf16[64,256]{1,0:T(8,128)(2,1)S(1)} %get-tuple-element.36), channel_id=1, source_target_pairs={{0,6},{1,7},{2,4},{3,5},{4,2},{5,3},{6,0},{7,1},{8,14},{9,15},{10,... | collective-permute-start | bytes 98312 | tf_op jit(solution)/shard_map/ppermute | solution.py:468
  18.2 4.6 %collective-permute-start.8 = (bf16[64,256]{1,0:T(8,128)(2,1)S(1)}, bf16[64,256]{1,0:T(8,128)(2,1)S(1)}, u32[]{:S(2)}, u32[]{:S(2)}) collective-permute-start(bf16[64,256]{1,0:T(8,128)(2,1)S(1)} %get-tuple-element.37), channel_id=1, source_target_pairs={{0,2},{1,3},{2,0},{3,1},{4,6},{5,7},{6,4},{7,5},{8,10},{9,11},{10,... | collective-permute-start | bytes 98312 | tf_op jit(solution)/shard_map/ppermute | solution.py:468
  23.1 1.6 %collective-permute-start.9 = (f32[32,2048]{1,0:T(8,128)S(1)}, f32[32,2048]{1,0:T(8,128)S(1)}, u32[]{:S(2)}, u32[]{:S(2)}) collective-permute-start(f32[32,2048]{1,0:T(8,128)S(1)} %get-tuple-element.39), channel_id=1, source_target_pairs={{0,1},{1,0},{2,3},{3,2},{4,5},{5,4},{6,7},{7,6},{8,9},{9,8},{10,11... | collective-permute-start | bytes 786440 | tf_op jit(solution)/shard_map/ppermute | solution.py:468
  24.7 1.4 %collective-permute-start.10 = (bf16[32,2048]{1,0:T(8,128)(2,1)S(1)}, bf16[32,2048]{1,0:T(8,128)(2,1)S(1)}, u32[]{:S(2)}, u32[]{:S(2)}) collective-permute-start(bf16[32,2048]{1,0:T(8,128)(2,1)S(1)} %act.1.mine_ref), channel_id=1, source_target_pairs={{0,1},{1,0},{2,3},{3,2},{4,5},{5,4},{6,7},{7,6},{8,9},{9,8},{10,11... | collective-permute-start | bytes 393224 | tf_op jit(solution)/shard_map/ppermute | solution.py:468
  26.6 4.0 %collective-permute-start.11 = (bf16[64,256]{1,0:T(8,128)(2,1)S(1)}, bf16[64,256]{1,0:T(8,128)(2,1)S(1)}, u32[]{:S(2)}, u32[]{:S(2)}) collective-permute-start(bf16[64,256]{1,0:T(8,128)(2,1)S(1)} %get-tuple-element.42), channel_id=1, source_target_pairs={{0,2},{1,3},{2,0},{3,1},{4,6},{5,7},{6,4},{7,5},{8,10},{9,11},{10,... | collective-permute-start | bytes 98312 | tf_op jit(solution)/shard_map/ppermute | solution.py:468
  27.1 16.7 %copy-start.3 = (f32[1024]{0:T(1024)S(1)}, f32[1024]{0:T(1024)}, u32[]{:S(2)}) copy-start(f32[1024]{0:T(1024)} %param.10) | copy-start | bytes 12292
  27.1 16.9 %copy-start = (bf16[1024,256]{1,0:T(8,128)(2,1)S(1)}, bf16[1024,256]{1,0:T(8,128)(2,1)}, u32[]{:S(2)}) copy-start(bf16[1024,256]{1,0:T(8,128)(2,1)} %coeff_ref.1) | copy-start | bytes 1572868
  27.2 16.9 %copy-start.1 = (s32[16]{0:T(128)S(1)}, s32[16]{0:T(128)}, u32[]{:S(2)}) copy-start(s32[16]{0:T(128)} %pad_ref.1) | copy-start | bytes 196
  27.2 16.9 %copy-start.2 = (f32[256]{0:T(256)S(1)}, f32[256]{0:T(256)}, u32[]{:S(2)}) copy-start(f32[256]{0:T(256)} %param.11) | copy-start | bytes 3076
  30.6 11.7 %collective-permute-start.14 = (bf16[128,256]{1,0:T(8,128)(2,1)S(1)}, bf16[128,256]{1,0:T(8,128)(2,1)S(1)}, u32[]{:S(2)}, u32[]{:S(2)}) collective-permute-start(bf16[128,256]{1,0:T(8,128)(2,1)S(1)} %assemble.2.near_ref), channel_id=1, source_target_pairs={{0,24},{8,16},{16,8},{24,0},{1,25},{9,17},{17,9},{25,1},{2,26},{10... | collective-permute-start | bytes 196616 | tf_op jit(solution)/shard_map/ppermute | solution.py:468
  33.6 5.8 %collective-permute-start.13 = (bf16[64,256]{1,0:T(8,128)(2,1)S(1)}, bf16[64,256]{1,0:T(8,128)(2,1)S(1)}, u32[]{:S(2)}, u32[]{:S(2)}) collective-permute-start(bf16[64,256]{1,0:T(8,128)(2,1)S(1)} %functions_more.5), channel_id=1, source_target_pairs={{0,6},{1,7},{2,4},{3,5},{4,2},{5,3},{6,0},{7,1},{8,14},{9,15},{10,... | collective-permute-start | bytes 98312 | tf_op jit(solution)/shard_map/ppermute | solution.py:468
  35.4 4.8 %collective-permute-start.12 = (bf16[64,256]{1,0:T(8,128)(2,1)S(1)}, bf16[64,256]{1,0:T(8,128)(2,1)S(1)}, u32[]{:S(2)}, u32[]{:S(2)}) collective-permute-start(bf16[64,256]{1,0:T(8,128)(2,1)S(1)} %functions_more.4), channel_id=1, source_target_pairs={{0,4},{1,5},{2,6},{3,7},{4,0},{5,1},{6,2},{7,3},{8,12},{9,13},{10,... | collective-permute-start | bytes 98312 | tf_op jit(solution)/shard_map/ppermute | solution.py:468
  35.4 10.0 %collective-permute-start.15 = (bf16[128,256]{1,0:T(8,128)(2,1)S(1)}, bf16[128,256]{1,0:T(8,128)(2,1)S(1)}, u32[]{:S(2)}, u32[]{:S(2)}) collective-permute-start(bf16[128,256]{1,0:T(8,128)(2,1)S(1)} %assemble.2.near_ref), channel_id=1, source_target_pairs={{0,8},{8,0},{16,24},{24,16},{1,9},{9,1},{17,25},{25,17},{2,10},{10... | collective-permute-start | bytes 196616 | tf_op jit(solution)/shard_map/ppermute | solution.py:468
  36.0 9.4 %collective-permute-start.16 = (bf16[128,256]{1,0:T(8,128)(2,1)S(1)}, bf16[128,256]{1,0:T(8,128)(2,1)S(1)}, u32[]{:S(2)}, u32[]{:S(2)}) collective-permute-start(bf16[128,256]{1,0:T(8,128)(2,1)S(1)} %assemble.2.near_ref), channel_id=1, source_target_pairs={{0,16},{8,24},{16,0},{24,8},{1,17},{9,25},{17,1},{25,9},{2,18},{10... | collective-permute-start | bytes 196616 | tf_op jit(solution)/shard_map/ppermute | solution.py:468
  40.3 6.4 %collective-permute-start.17 = (bf16[128,256]{1,0:T(8,128)(2,1)S(1)}, bf16[128,256]{1,0:T(8,128)(2,1)S(1)}, u32[]{:S(2)}, u32[]{:S(2)}) collective-permute-start(bf16[128,256]{1,0:T(8,128)(2,1)S(1)} %assemble.3.refs_0_), channel_id=1, source_target_pairs={{0,24},{8,16},{16,8},{24,0},{1,25},{9,17},{17,9},{25,1},{2,26},{10... | collective-permute-start | bytes 196616 | tf_op jit(solution)/shard_map/ppermute | solution.py:468
  40.8 5.8 %collective-permute-start.18 = (bf16[128,256]{1,0:T(8,128)(2,1)S(1)}, bf16[128,256]{1,0:T(8,128)(2,1)}, u32[]{:S(2)}, u32[]{:S(2)}) collective-permute-start(bf16[128,256]{1,0:T(8,128)(2,1)S(1)} %assemble.3.refs_0_), channel_id=1, source_target_pairs={{0,8},{8,0},{16,24},{24,16},{1,9},{9,1},{17,25},{25,17},{2,10},{10... | collective-permute-start | bytes 196616 | tf_op jit(solution)/shard_map/ppermute | solution.py:468
  42.3 6.1 %collective-permute-start.19 = (bf16[128,256]{1,0:T(8,128)(2,1)S(1)}, bf16[128,256]{1,0:T(8,128)(2,1)}, u32[]{:S(2)}, u32[]{:S(2)}) collective-permute-start(bf16[128,256]{1,0:T(8,128)(2,1)S(1)} %assemble.3.refs_0_), channel_id=1, source_target_pairs={{0,16},{8,24},{16,0},{24,8},{1,17},{9,25},{17,1},{25,9},{2,18},{10... | collective-permute-start | bytes 196616 | tf_op jit(solution)/shard_map/ppermute | solution.py:468
